TPU v7x, 256 devices: a whole 4x4x8 slice. The times are simulated.
256 devices in a mesh: rep: 32 (over z_hi, y, core), fsdp: 8 (over z_lo, x).
Axes of the slice: x: 4, y: 4, z: 8 (z_hi: 4, z_lo: 2; z = z_hi * 2 + z_lo), core: 2. Of those that a mesh axis runs over, the one named last changes fastest.
Arguments:
- inputs: bfloat16 [32, 2, 2048, 4096], P('rep', None, 'fsdp'), may hold values from -6 to 6
- queries: bfloat16 [32, 2, 2048, 4096], P('rep', None, 'fsdp'), may hold values from -6 to 6
- keys: bfloat16 [32, 2, 2048, 512], P('rep', None, 'fsdp'), may hold values from -6 to 6
- value_w: bfloat16 [32, 512, 4096], P('rep', None, 'fsdp'), may hold values from -0.09375 to 0.09375
- anchor: float32 [512, 4096], P('rep', 'fsdp'), may hold values from -0.09375 to 0.09375
- momentum: float32 [512, 4096], P('rep', 'fsdp'), may hold values from -0.3 to 0.3
- prev_delta: bfloat16 [32, 512, 4096], P('rep', None, 'fsdp'), may hold values from -1.1953125 to 1.1953125
Outputs:
- value_out: bfloat16 [32, 512, 4096], P('rep', None, 'fsdp')
- anchor_out: float32 [512, 4096], P('rep', 'fsdp')
- momentum_out: float32 [512, 4096], P('rep', 'fsdp')
- delta_out: bfloat16 [32, 512, 4096], P('rep', None, 'fsdp')
All inputs are finite; a program needn't handle non-finite values.
Results may differ from a plain program's by a relative error of at most 0.029.
Values may be sent and summed in bfloat16 or wider, within the bound.
No kernel may reach another device: no remote copies, remote signals or barrier semaphores. Data moves between devices by JAX's collectives and lax.ppermute only.
A program may use at most 128 MiB of HBM per device.

v0:
```python
import functools
import math

import jax
import jax.numpy as jnp
from jax import lax
from jax.experimental import pallas as pl
from jax.experimental.pallas import tpu as pltpu
from jax.sharding import PartitionSpec as P

HD = 128
HQ = 32
KVH = 4
GROUP = HQ // KVH
STEPS = 2
CHUNKS = 2
NX = 4
NZ = 2

inner_rate = 0.5
outer_rate = 0.7
outer_mu = 0.9
mix_share = 0.5

BF = jnp.bfloat16
F32 = jnp.float32
NT = (((1,), (1,)), ((), ()))
NN = (((1,), (0,)), ((), ()))
VMEM_LIMIT = 16 * 1024 * 1024
ATTENTION_LIMIT = 60 * 1024 * 1024
TOKEN = ((8, 128), F32)
COST = pl.CostEstimate(flops=1000, bytes_accessed=1000, transcendentals=0)

X_PLUS = [(i, i // NX * NX + (i % NX + 1) % NX) for i in range(NX * NZ)]
X_MINUS = [(i, i // NX * NX + (i % NX + NX - 1) % NX) for i in range(NX * NZ)]
Z_SWAP = [(i, (i + NX) % (NX * NZ)) for i in range(NX * NZ)]
NY = 4
NZH = 4
N_REP = NZH * NY * 2


def dot(a, b, dims):
    return lax.dot_general(a, b, dims, preferred_element_type=F32)


def attention_kernel(_, t_in, q_ref, k_ref, x_ref, m_ref, nt_ref, t_out, w_low, w_high, targets):
    t_out[...] = t_in[...]
    length = k_ref.shape[0]
    half = length // 2
    k_low, k_high = k_ref[:half, :], k_ref[half:, :]
    u_at = lax.broadcasted_iota(jnp.int32, (half, half), 0)
    t_at = lax.broadcasted_iota(jnp.int32, (half, half), 1)
    keep = u_at <= t_at
    row_at = lax.broadcasted_iota(jnp.int32, (length, HD), 0)
    factor = math.log2(math.e) / math.sqrt(HD)
    for g in range(GROUP):
        cols = slice(g * HD, (g + 1) * HD)
        q_low, q_high = q_ref[:half, cols], q_ref[half:, cols]
        s_low = jnp.where(keep, dot(k_low, q_low, NT), -1e30)
        s_top = dot(k_low, q_high, NT)
        s_diag = jnp.where(keep, dot(k_high, q_high, NT), -1e30)
        peak = jnp.max(s_low, axis=0, keepdims=True)
        e_low = jnp.exp2((s_low - peak) * factor)
        w_low[:, cols] = (e_low * (1.0 / jnp.sum(e_low, axis=0, keepdims=True))).astype(BF)
        peak = jnp.max(jnp.maximum(s_top, s_diag), axis=0, keepdims=True)
        e_top = jnp.exp2((s_top - peak) * factor)
        e_diag = jnp.exp2((s_diag - peak) * factor)
        share = 1.0 / jnp.sum(e_top + e_diag, axis=0, keepdims=True)
        w_high[:half, cols] = (e_top * share).astype(BF)
        w_high[half:, cols] = (e_diag * share).astype(BF)
        shifted = pltpu.roll(x_ref[:, cols].astype(F32), length - 1, 0)
        target = jnp.where(row_at == length - 1, 0.0, shifted).astype(BF)
        targets[0, g * half : (g + 1) * half, :] = target[:half]
        targets[1, g * half : (g + 1) * half, :] = target[half:]
    m_high = dot(w_high[...], w_high[...], NT)
    m_low = dot(w_low[...], w_low[...], NT)
    m_ref[:half, :half] = (m_high[:half, :half] + m_low).astype(BF)
    m_ref[:half, half:] = m_high[:half, half:].astype(BF)
    m_ref[half:, :] = m_high[half:, :].astype(BF)
    n_high = dot(w_high[...], targets[1], NN)
    n_low = dot(w_low[...], targets[0], NN)
    nt_ref[:, :half] = (n_high[:half] + n_low).T
    nt_ref[:, half:] = n_high[half:].T


def attention_matrices(before, token, queries, keys, rows, step):
    length = rows.shape[2]
    half = length // 2
    wide = GROUP * HD
    m_part, nt_part, token = pl.pallas_call(
        attention_kernel,
        grid=(KVH,),
        in_specs=[
            pl.BlockSpec(memory_space=pl.ANY),
            pl.BlockSpec(TOKEN[0], lambda j: (0, 0)),
            pl.BlockSpec((None, None, length, wide), lambda j: (0, step, 0, j)),
            pl.BlockSpec((None, None, length, HD), lambda j: (0, step, 0, j)),
            pl.BlockSpec((None, None, length, wide), lambda j: (0, step, 0, j)),
        ],
        out_specs=[
            pl.BlockSpec((None, length, length), lambda j: (j, 0, 0)),
            pl.BlockSpec((HD, length), lambda j: (j, 0)),
            pl.BlockSpec(TOKEN[0], lambda j: (0, 0)),
        ],
        out_shape=[
            jax.ShapeDtypeStruct((KVH, length, length), BF),
            jax.ShapeDtypeStruct((KVH * HD, length), F32),
            jax.ShapeDtypeStruct(*TOKEN),
        ],
        scratch_shapes=[
            pltpu.VMEM((half, GROUP * half), BF),
            pltpu.VMEM((length, GROUP * half), BF),
            pltpu.VMEM((2, GROUP * half, HD), BF),
        ],
        compiler_params=pltpu.CompilerParams(vmem_limit_bytes=ATTENTION_LIMIT),
        cost_estimate=COST,
        name="attention_matrices",
    )(before, token, queries, keys, rows)
    return (m_part, nt_part), token


VMEM = pl.BlockSpec(memory_space=pltpu.VMEM)
SMEM = pl.BlockSpec(memory_space=pltpu.SMEM)


def ordered(body, name, x_id, token, operands, outs):
    def kernel(x_at, token_in, *refs):
        body(x_at[0], *refs[:-1])
        refs[-1][...] = token_in[...]

    results = pl.pallas_call(
        kernel,
        in_specs=[SMEM] + [VMEM] * (1 + len(operands)),
        out_specs=[VMEM] * (len(outs) + 1),
        out_shape=[jax.ShapeDtypeStruct(*o) for o in [*outs, TOKEN]],
        compiler_params=pltpu.CompilerParams(vmem_limit_bytes=VMEM_LIMIT),
        cost_estimate=COST,
        name=name,
    )(x_id, token, *operands)
    return results[:-1], results[-1]


def own_columns(x_id, k, width):
    return pl.ds(pl.multiple_of((x_id + k) % NX * width, width), width)


def value_piece(x_id, own, left, right, opp, rows):
    width = own.shape[1]
    acc = None
    for w_part, k in ((own, 0), (right, 1), (opp, 2), (left, 3)):
        term = dot(w_part[...], rows[:, own_columns(x_id, k, width)], NT)
        acc = term if acc is None else acc + term
    return acc


def value_body(x_id, own, left, right, opp, *refs):
    out, first = refs[-1], 0
    for other in refs[:-1]:
        cols = slice(first, first + other.shape[0])
        out[:, cols] = value_piece(x_id, own, left, right, opp, other).astype(BF)
        first = cols.stop


def grad_body(first, x_id, own, left, right, opp, mine, got, m_ref, nt_ref, out):
    value = value_piece(x_id, own, left, right, opp, mine)
    value = (value + got[...].astype(F32)).astype(BF)
    for j in range(out.shape[0] // HD):
        rows = slice(j * HD, (j + 1) * HD)
        at = first + j
        minus = nt_ref[at * HD : (at + 1) * HD, :]
        out[rows, :] = (dot(value[rows, :], m_ref[at], NN) - minus).astype(BF)


def sum_piece(x_id, k, width, g_mine, g_other, rows):
    cols = own_columns(x_id, k, width)
    total = dot(g_mine[...], rows[0][:, cols], NN)
    first = 0
    for other in rows[1:]:
        tokens = slice(first, first + other.shape[0])
        total = total + dot(g_other[:, tokens], other[:, cols], NN)
        first = tokens.stop
    return total


def sum_body(side, x_id, g_mine, g_other, *refs):
    *rows, opp, plain = refs
    width = opp.shape[1]
    for k, dst in ((2, opp), (4 - side, plain)):
        dst[...] = sum_piece(x_id, k, width, g_mine, g_other, rows).astype(BF)


def add_body(side, x_id, g_mine, g_other, *refs):
    *rows, opp_in, out = refs
    term = sum_piece(x_id, side, out.shape[1], g_mine, g_other, rows)
    out[...] = (term + opp_in[...].astype(F32)).astype(BF)


def step_body(rate, x_id, g_mine, g_other, *refs):
    *rows, plain_in, added_in, w_ref, out = refs
    total = sum_piece(x_id, 0, out.shape[1], g_mine, g_other, rows)
    total = total + plain_in[...].astype(F32) + added_in[...].astype(F32)
    out[...] = (w_ref[...].astype(F32) - rate * total).astype(BF)


def own_body(x_id, g_mine, g_other, *refs):
    *rows, out = refs
    out[...] = sum_piece(x_id, 0, out.shape[1], g_mine, g_other, rows)


def last_body(rate, n, x_id, *refs):
    *rows_refs, both, value_out, delta_out = refs[5 * n :]
    n_kv, (n_y, _, n_z, height, _) = value_out.shape[1] // n, both.shape
    near = [[both[y, i, z] for z in range(n_z) for y in range(n_y)] for i in (0, 1)]
    for c in range(n):
        g_mine, g_other, plain_in, added_in, w_ref = refs[5 * c : 5 * c + 5]
        total = sum_piece(x_id, 0, w_ref.shape[1], g_mine, g_other, rows_refs)
        total = total + plain_in[...].astype(F32) + added_in[...].astype(F32)
        inner = (w_ref[...].astype(F32) - rate * total).astype(BF).astype(F32)
        rows = slice(c * n_kv, (c + 1) * n_kv)
        here = slice(c * n_kv // height, (c + 1) * n_kv // height)
        new, old = (jnp.concatenate(v[here], axis=0).astype(F32) for v in near)
        value_out[0, rows, :] = (mix_share * inner + (1.0 - mix_share) * new).astype(BF)
        delta_out[0, rows, :] = (old - inner).astype(BF)


def send(value, perm):
    return lax.ppermute(value, "fsdp", perm)


def gather_x(side, own, gate=None):
    left = send(own, X_PLUS)
    right = send(own, X_MINUS)
    near, perm = (left, X_PLUS) if side == 1 else (right, X_MINUS)
    return own, left, right, send(near if gate is None else gated(near, gate), perm)


def gated(value, token):
    return lax.optimization_barrier((value, token))[0]


def inner_steps(inputs, queries, keys, value_w, outer):
    length, width = inputs.shape[2:]
    half_width = width // NZ
    at = lax.axis_index("fsdp")
    x_id = (at % NX).astype(jnp.int32).reshape(1)
    z_id = at // NX
    rate = inner_rate / (length * NX * NZ)
    n_kv = value_w.shape[1] // CHUNKS
    firsts = [c * n_kv for c in range(CHUNKS)]
    sides = [1, 3]
    chunks = range(CHUNKS)
    there = [X_PLUS, X_MINUS]
    back = [X_MINUS, X_PLUS]
    tokens_bf = ((n_kv, length), BF)
    piece = ((n_kv, width // (NX * NZ)), BF)
    piece_f32 = (piece[0], F32)

    def columns(rows, step, half):
        start = (0, step, 0, half * half_width)
        return lax.dynamic_slice(rows, start, (1, 1, length, half_width))[0, 0]

    def swap_rows(rows, step, part):
        start = (0, step, part * length // 2, (1 - z_id) * half_width)
        away = lax.dynamic_slice(rows, start, (1, 1, length // 2, half_width))
        return send(away[0, 0], Z_SWAP)

    away = columns(inputs, 0, 1 - z_id)
    other = [send(away, Z_SWAP)]
    w_now = [value_w[0, f : f + n_kv] for f in firsts]
    token = jnp.zeros(*TOKEN)
    matrices = [None] * STEPS
    matrices[0], token = attention_matrices(away, token, queries, keys, inputs, 0)
    gathered = [gather_x(sides[c], w_now[c], token) for c in chunks]
    mine = columns(gated(inputs, token), 0, z_id)
    matrices[1], token = attention_matrices(away, token, queries, keys, inputs, 1)
    for step in range(STEPS):
        got, g_mine, g_other, opp_in, plain_in, added_in = ([None] * CHUNKS for _ in range(6))
        for c in chunks:
            (out,), token = ordered(
                value_body, "value_partial", x_id, token, [*gathered[c], *other], [tokens_bf]
            )
            got[c] = send(out, Z_SWAP)
        if step == 0:
            outer.send(token)
        for c in chunks:
            (g_mine[c],), token = ordered(
                functools.partial(grad_body, firsts[c] // HD),
                "grad_value",
                x_id,
                token,
                [*gathered[c], mine, got[c], *matrices[step]],
                [tokens_bf],
            )
            g_other[c] = send(g_mine[c], Z_SWAP)
        operands = [[g_mine[c], g_other[c], mine, *other] for c in chunks]
        for c in chunks:
            body = functools.partial(sum_body, sides[c])
            (opp, plain), token = ordered(body, "sum_partial", x_id, token, operands[c], [piece, piece])
            opp_in[c] = send(opp, there[c])
            plain_in[c] = send(plain, back[c])
        for c in chunks:
            body = functools.partial(add_body, sides[c])
            (added,), token = ordered(body, "sum_added", x_id, token, [*operands[c], opp_in[c]], [piece])
            added_in[c] = send(added, there[c])
        if step + 1 == STEPS:
            break
        outer.send(token)
        next_mine = columns(gated(inputs, token), step + 1, z_id)
        next_other = [swap_rows(gated(inputs, token), step + 1, 0)]
        for c in chunks:
            (w_now[c],), token = ordered(
                functools.partial(step_body, rate),
                "sum_step",
                x_id,
                token,
                [*operands[c], plain_in[c], added_in[c], w_now[c]],
                [piece],
            )
            gathered[c] = gather_x(sides[c], w_now[c])
        next_other.append(swap_rows(gated(inputs, token), step + 1, 1))
        mine, other = next_mine, next_other
    args = []
    for c in chunks:
        args += [g_mine[c], g_other[c], plain_in[c], added_in[c], w_now[c]]
    args += [mine, *other]
    both, momentum_out, anchor_out = next(outer)
    whole = ((1, *value_w.shape[1:]), BF)
    (value_out, delta_out), token = ordered(
        functools.partial(last_body, rate, CHUNKS), "last_step", x_id, token, [*args, both], [whole, whole]
    )
    return value_out, anchor_out, momentum_out, delta_out


def outer_stages(anchor, momentum, prev_delta):
    height, width = anchor.shape
    rep = lax.axis_index("rep")
    low = rep % 2 == 0
    along_y = [[r for r in range(N_REP) if r // 8 == g // 2 and r % 2 == g % 2] for g in range(8)]
    along_z = [[r for r in range(N_REP) if r % 8 == g] for g in range(8)]

    def gather(value, groups):
        return lax.all_gather(value, "rep", axis=0, axis_index_groups=groups)

    parts = prev_delta[0].reshape(NZH, NY, 2 * height, width).transpose(1, 0, 2, 3)
    sums = lax.psum_scatter(
        parts.reshape(N_REP * height, width),
        "rep",
        scatter_dimension=0,
        axis_index_groups=along_y,
        tiled=True,
    )
    owns = jnp.concatenate([anchor.astype(BF), momentum.astype(BF)], axis=0)
    token = yield
    rows = sums.shape[0]
    here = gated(jnp.concatenate([sums, owns], axis=0), token)
    there = lax.ppermute(here, "rep", [(r, r ^ 1) for r in range(N_REP)])
    sums = (here[:rows].astype(F32) + there[:rows].astype(F32)).astype(BF)
    first, second = jnp.where(low, here[rows:], there[rows:]), jnp.where(low, there[rows:], here[rows:])
    fill = jnp.zeros((2 * height, width), BF)
    near = gather(jnp.concatenate([sums, first, second, fill, fill], axis=0), along_z)
    token = yield
    near = gated(near, token)
    average = jnp.sum(near[:, :rows].astype(F32), axis=0) / N_REP
    owns = near[:, rows : rows + 4 * height].reshape(NZH, 2, 2, height, width).astype(F32)
    owns = owns.transpose(2, 0, 1, 3, 4).reshape(2, rows, width)
    momentum_new = outer_mu * owns[1] + average
    anchor_new = owns[0] - outer_rate * (outer_mu * momentum_new + average)
    both = gather(jnp.stack([anchor_new, owns[0]], axis=0).astype(BF), along_y)
    at = (rep // 8 * 2 + rep % 2) * height
    average = lax.dynamic_slice_in_dim(average, at, height, 0)
    momentum_out = outer_mu * momentum + average
    anchor_out = anchor - outer_rate * (outer_mu * momentum_out + average)
    yield
    yield both.reshape(NY, 2, NZH, 2 * height, width), momentum_out, anchor_out


def shards(inputs, queries, keys, value_w, anchor, momentum, prev_delta):
    outer = outer_stages(anchor, momentum, prev_delta)
    next(outer)
    return inner_steps(inputs, queries, keys, value_w, outer)


def solution(mesh):
    placed = (
        P("rep", None, "fsdp", None),
        P("rep", None, "fsdp", None),
        P("rep", None, "fsdp", None),
        P("rep", None, "fsdp"),
        P("rep", "fsdp"),
        P("rep", "fsdp"),
        P("rep", None, "fsdp"),
    )
    return jax.shard_map(
        shards,
        mesh=mesh,
        in_specs=placed,
        out_specs=(
            P("rep", None, "fsdp"),
            P("rep", "fsdp"),
            P("rep", "fsdp"),
            P("rep", None, "fsdp"),
        ),
        check_vma=False,
    )
```

profile of v0, /device:TPU:94, one launch (start us, length us, event | category | flops | bytes accessed | tf_op | source)
XLA Modules:
  0.0 159.5 jit_solution(17270277604433987622)
XLA Ops:
  7.2 2.3 %dynamic-slice_bitcast_fusion.2._ = bf16[256,2048]{1,0:T(8,128)(2,1)} fusion(bf16[1,2,256,4096]{3,2,1,0:T(8,128)(2,1)} %x_ref.3, s32[]{:T(128)S(6)} %select_n.46), kind=kLoop, calls=%fused_computation.3 | loop fusion | bytes 2097156 | tf_op jit(solution)/shard_map/squeeze | solution.py:260
  9.5 1.9 %collective-permute-start.3 = (bf16[256,2048]{1,0:T(8,128)(2,1)}, bf16[256,2048]{1,0:T(8,128)(2,1)S(1)}, u32[]{:S(2)}, u32[]{:S(2)}) collective-permute-start(bf16[256,2048]{1,0:T(8,128)(2,1)} %dynamic-slice_bitcast_fusion.2._), channel_id=1, source_target_pairs={{0,4},{1,5},{2,6},{3,7},{4,0},{5,1},{6,2},{7,3},{8,12},{9,13},{10,... | collective-permute-start | bytes 3145736 | tf_op jit(solution)/shard_map/ppermute | solution.py:227
  11.5 1.9 %copy.12 = bf16[4,4,32,512]{3,2,1,0:T(8,128)(2,1)} copy(bf16[4,4,32,512]{3,2,0,1:T(8,128)(2,1)} %bitcast.52) | data formatting | bytes 1048576 | tf_op jit(solution)/shard_map/transpose | solution.py:344
  13.4 1.1 slice_bitcast_fusion
  15.0 1.5 collective-permute-start.5
  16.6 0.8 collective-permute-start.1
  18.0 7.8 %attention_matrices.2 = (bf16[4,256,256]{2,1,0:T(8,128)(2,1)}, f32[512,256]{1,0:T(8,128)}, f32[8,128]{1,0:T(8,128)}) custom-call(bf16[256,2048]{1,0:T(8,128)(2,1)} %dynamic-slice_bitcast_fusion.2._, f32[8,128]{1,0:T(8,128)} %broadcast_in_dim.3.t_in, bf16[1,2,256,4096]{3,2,1,0:T(8,128)(2,1)} %q_ref.3, bf16[1,2,256,512]{3,2,1,0:T(8,128)(2,1)} %k_ref.3, ...), custom_call_target="tpu_custom_call" | custom-call | flops 1000 | bytes 1000 | tf_op jit(solution)/shard_map/attention_matrices/pallas_call | solution.py:90
  25.8 2.5 %collective-permute-start.2 = (bf16[256,512]{1,0:T(8,128)(2,1)S(1)}, bf16[256,512]{1,0:T(8,128)(2,1)}, u32[]{:S(2)}, u32[]{:S(2)}) collective-permute-start(bf16[256,512]{1,0:T(8,128)(2,1)S(1)} %collective-permute-done.refs_1_), channel_id=1, source_target_pairs={{0,1},{1,2},{2,3},{3,0},{4,5},{5,6},{6,7},{7,4},{8,9},{9,10},{10,1... | collective-permute-start | bytes 786440 | tf_op jit(solution)/shard_map/ppermute | solution.py:227
  28.8 1.5 collective-permute-start.6
  30.4 7.8 %attention_matrices.3 = (bf16[4,256,256]{2,1,0:T(8,128)(2,1)}, f32[512,256]{1,0:T(8,128)}, f32[8,128]{1,0:T(8,128)}) custom-call(bf16[256,2048]{1,0:T(8,128)(2,1)} %dynamic-slice_bitcast_fusion.2._, f32[8,128]{1,0:T(8,128)} %get-tuple-element.59.t_in, bf16[1,2,256,4096]{3,2,1,0:T(8,128)(2,1)} %q_ref.3, bf16[1,2,256,512]{3,2,1,0:T(8,128)(2,1)} %k_ref.3, ...), custom_call_target="tpu_custom_call" | custom-call | flops 1000 | bytes 1000 | tf_op jit(solution)/shard_map/attention_matrices/pallas_call | solution.py:90
  40.1 1.5 value_partial.4
  42.3 1.4 value_partial.5
  43.7 1.6 %pad_maximum_fusion.1 = bf16[160,512]{1,0:T(8,128)(2,1)} fusion(bf16[16,512]{1,0:T(8,128)(2,1)} %convert_element_type.31, bf16[16,512]{1,0:T(8,128)(2,1)} %convert_element_type.30, bf16[128,512]{1,0:T(8,128)(2,1)} %reduce-scatter.2.cloned.1.call-done), kind=kLoop, calls=%fused_computation.19 | loop fusion | flops 491520 | bytes 327680 | tf_op jit(solution)/shard_map/concatenate | solution.py:355
  45.4 1.7 %collective-permute-done.35 = bf16[160,512]{1,0:T(8,128)(2,1)} collective-permute-done((bf16[160,512]{1,0:T(8,128)(2,1)}, bf16[160,512]{1,0:T(8,128)(2,1)}, u32[]{:S(2)}, u32[]{:S(2)}) %collective-permute-start.35) | collective-permute-done | bytes 163872 | tf_op jit(solution)/shard_map/ppermute | solution.py:356
  47.1 1.0 add_convert_fusion
  48.1 0.8 broadcast_select_fusion.1
  48.9 0.8 maximum_maximum_fusion
  49.9 1.9 %collective-permute-start.8 = (bf16[256,256]{1,0:T(8,128)(2,1)S(1)}, bf16[256,256]{1,0:T(8,128)(2,1)S(1)}, u32[]{:S(2)}, u32[]{:S(2)}) collective-permute-start(bf16[256,256]{1,0:T(8,128)(2,1)S(1)} %get-tuple-element.70), channel_id=1, source_target_pairs={{0,4},{1,5},{2,6},{3,7},{4,0},{5,1},{6,2},{7,3},{8,12},{9,13},{10,... | collective-permute-start | bytes 393224 | tf_op jit(solution)/shard_map/ppermute | solution.py:227
  51.9 1.3 dynamic-slice_bitcast_fusion.1.refs_4_.refs_2_
  53.2 3.2 %collective-permute-done.7.refs_5_ = bf16[256,256]{1,0:T(8,128)(2,1)S(1)} collective-permute-done((bf16[256,256]{1,0:T(8,128)(2,1)}, bf16[256,256]{1,0:T(8,128)(2,1)S(1)}, u32[]{:S(2)}, u32[]{:S(2)}) %collective-permute-start.7) | collective-permute-done | bytes 131104 | tf_op jit(solution)/shard_map/ppermute | solution.py:227
  56.4 1.7 %grad_value.4 = (bf16[256,256]{1,0:T(8,128)(2,1)S(1)}, f32[8,128]{1,0:T(8,128)S(1)}) custom-call(s32[1]{0:T(128)} %bitcast.x_at, f32[8,128]{1,0:T(8,128)S(1)} %get-tuple-element.64.token_in, bf16[256,512]{1,0:T(8,128)(2,1)S(1)} %get-tuple-element.119.refs_0_.refs_6_, bf16[256,512]{1,0:T(8,128)(2,1)S(1)} %collective-permute-done.refs_1_, ...), custom_call_target="tpu_custom_call" | custom-call | flops 1000 | bytes 1000 | tf_op jit(solution)/shard_map/grad_value/pallas_call | solution.py:131
  58.5 1.6 %grad_value.5 = (bf16[256,256]{1,0:T(8,128)(2,1)S(1)}, f32[8,128]{1,0:T(8,128)S(1)}) custom-call(s32[1]{0:T(128)} %bitcast.x_at, f32[8,128]{1,0:T(8,128)S(1)} %get-tuple-element.69.token_in, bf16[256,512]{1,0:T(8,128)(2,1)S(1)} %get-tuple-element.118.refs_0_.refs_6_, bf16[256,512]{1,0:T(8,128)(2,1)S(1)} %collective-permute-done.4.refs_1_, ...), custom_call_target="tpu_custom_call" | custom-call | flops 1000 | bytes 1000 | tf_op jit(solution)/shard_map/grad_value/pallas_call | solution.py:131
  60.1 2.0 %collective-permute-start.10 = (bf16[256,256]{1,0:T(8,128)(2,1)S(1)}, bf16[256,256]{1,0:T(8,128)(2,1)S(1)}, u32[]{:S(2)}, u32[]{:S(2)}) collective-permute-start(bf16[256,256]{1,0:T(8,128)(2,1)S(1)} %get-tuple-element.74.refs_0_), channel_id=1, source_target_pairs={{0,4},{1,5},{2,6},{3,7},{4,0},{5,1},{6,2},{7,3},{8,12},{9,13},{10,... | collective-permute-start | bytes 393224 | tf_op jit(solution)/shard_map/ppermute | solution.py:227
  62.1 2.5 %collective-permute-done.9.refs_1_ = bf16[256,256]{1,0:T(8,128)(2,1)S(1)} collective-permute-done((bf16[256,256]{1,0:T(8,128)(2,1)S(1)}, bf16[256,256]{1,0:T(8,128)(2,1)S(1)}, u32[]{:S(2)}, u32[]{:S(2)}) %collective-permute-start.9) | collective-permute-done | bytes 131104 | tf_op jit(solution)/shard_map/ppermute | solution.py:227
  65.1 1.9 %collective-permute-start.11 = (bf16[256,512]{1,0:T(8,128)(2,1)S(1)}, bf16[256,512]{1,0:T(8,128)(2,1)S(1)}, u32[]{:S(2)}, u32[]{:S(2)}) collective-permute-start(bf16[256,512]{1,0:T(8,128)(2,1)S(1)} %get-tuple-element.76), channel_id=1, source_target_pairs={{0,1},{1,2},{2,3},{3,0},{4,5},{5,6},{6,7},{7,4},{8,9},{9,10},{10,1... | collective-permute-start | bytes 786440 | tf_op jit(solution)/shard_map/ppermute | solution.py:227
  67.0 4.8 %collective-permute-done.10.refs_1_ = bf16[256,256]{1,0:T(8,128)(2,1)S(1)} collective-permute-done((bf16[256,256]{1,0:T(8,128)(2,1)S(1)}, bf16[256,256]{1,0:T(8,128)(2,1)S(1)}, u32[]{:S(2)}, u32[]{:S(2)}) %collective-permute-start.10) | collective-permute-done | bytes 131104 | tf_op jit(solution)/shard_map/ppermute | solution.py:227
  72.4 0.8 collective-permute-done.11.refs_4_
  73.5 2.5 %collective-permute-start.14 = (bf16[256,512]{1,0:T(8,128)(2,1)S(1)}, bf16[256,512]{1,0:T(8,128)(2,1)S(1)}, u32[]{:S(2)}, u32[]{:S(2)}) collective-permute-start(bf16[256,512]{1,0:T(8,128)(2,1)S(1)} %get-tuple-element.81), channel_id=1, source_target_pairs={{0,1},{1,2},{2,3},{3,0},{4,5},{5,6},{6,7},{7,4},{8,9},{9,10},{10,1... | collective-permute-start | bytes 786440 | tf_op jit(solution)/shard_map/ppermute | solution.py:227
  76.0 1.9 %collective-permute-start.15 = (bf16[256,512]{1,0:T(8,128)(2,1)S(1)}, bf16[256,512]{1,0:T(8,128)(2,1)S(1)}, u32[]{:S(2)}, u32[]{:S(2)}) collective-permute-start(bf16[256,512]{1,0:T(8,128)(2,1)S(1)} %get-tuple-element.83), channel_id=1, source_target_pairs={{0,1},{1,2},{2,3},{3,0},{4,5},{5,6},{6,7},{7,4},{8,9},{9,10},{10,1... | collective-permute-start | bytes 786440 | tf_op jit(solution)/shard_map/ppermute | solution.py:227
  77.9 4.7 %collective-permute-done.12.refs_4_ = bf16[256,512]{1,0:T(8,128)(2,1)S(1)} collective-permute-done((bf16[256,512]{1,0:T(8,128)(2,1)S(1)}, bf16[256,512]{1,0:T(8,128)(2,1)S(1)}, u32[]{:S(2)}, u32[]{:S(2)}) %collective-permute-start.12) | collective-permute-done | bytes 262176 | tf_op jit(solution)/shard_map/ppermute | solution.py:227
  83.0 1.9 %dynamic-slice_bitcast_fusion.4 = bf16[128,2048]{1,0:T(8,128)(2,1)} fusion(bf16[1,2,256,4096]{3,2,1,0:T(8,128)(2,1)} %x_ref.3, s32[]{:T(128)S(6)} %select_n.46), kind=kLoop, calls=%fused_computation.6 | loop fusion | bytes 1048580 | tf_op jit(solution)/shard_map/squeeze | solution.py:265
  85.0 2.9 %collective-permute-done.13.refs_4_ = bf16[256,512]{1,0:T(8,128)(2,1)S(1)} collective-permute-done((bf16[256,512]{1,0:T(8,128)(2,1)S(1)}, bf16[256,512]{1,0:T(8,128)(2,1)S(1)}, u32[]{:S(2)}, u32[]{:S(2)}) %collective-permute-start.13) | collective-permute-done | bytes 262176 | tf_op jit(solution)/shard_map/ppermute | solution.py:227
  88.6 1.7 %collective-permute-start.18 = (bf16[256,512]{1,0:T(8,128)(2,1)S(1)}, bf16[256,512]{1,0:T(8,128)(2,1)}, u32[]{:S(2)}, u32[]{:S(2)}) collective-permute-start(bf16[256,512]{1,0:T(8,128)(2,1)S(1)} %get-tuple-element.86.refs_0_.refs_4_), channel_id=1, source_target_pairs={{0,3},{1,0},{2,1},{3,2},{4,7},{5,4},{6,5},{7,6},{8,11},{9,8},{10,9... | collective-permute-start | bytes 786440 | tf_op jit(solution)/shard_map/ppermute | solution.py:227
  90.4 2.8 %collective-permute-done.16.refs_5_ = bf16[256,512]{1,0:T(8,128)(2,1)S(1)} collective-permute-done((bf16[256,512]{1,0:T(8,128)(2,1)S(1)}, bf16[256,512]{1,0:T(8,128)(2,1)S(1)}, u32[]{:S(2)}, u32[]{:S(2)}) %collective-permute-start.16) | collective-permute-done | bytes 262176 | tf_op jit(solution)/shard_map/ppermute | solution.py:227
  93.5 1.9 %dynamic-slice_bitcast_fusion.3 = bf16[128,2048]{1,0:T(8,128)(2,1)} fusion(bf16[1,2,256,4096]{3,2,1,0:T(8,128)(2,1)} %x_ref.3, s32[]{:T(128)S(6)} %select_n.46), kind=kLoop, calls=%fused_computation.5 | loop fusion | bytes 1048580 | tf_op jit(solution)/shard_map/squeeze | solution.py:265
  95.4 1.0 slice.41
  96.6 1.1 convert_reduce_fusion
  98.6 3.3 %collective-permute-start.19 = (bf16[256,512]{1,0:T(8,128)(2,1)S(1)}, bf16[256,512]{1,0:T(8,128)(2,1)S(1)}, u32[]{:S(2)}, u32[]{:S(2)}) collective-permute-start(bf16[256,512]{1,0:T(8,128)(2,1)S(1)} %collective-permute-done.17.refs_1_), channel_id=1, source_target_pairs={{0,1},{1,2},{2,3},{3,0},{4,5},{5,6},{6,7},{7,4},{8,9},{9,10},{10,1... | collective-permute-start | bytes 786440 | tf_op jit(solution)/shard_map/ppermute | solution.py:227
  102.2 0.8 collective-permute-done.23.refs_2_
  103.0 0.9 collective-permute-start.24
  103.9 1.9 %collective-permute-done.19.refs_3_ = bf16[256,512]{1,0:T(8,128)(2,1)S(1)} collective-permute-done((bf16[256,512]{1,0:T(8,128)(2,1)S(1)}, bf16[256,512]{1,0:T(8,128)(2,1)S(1)}, u32[]{:S(2)}, u32[]{:S(2)}) %collective-permute-start.19) | collective-permute-done | bytes 262176 | tf_op jit(solution)/shard_map/ppermute | solution.py:227
  105.7 1.7 %collective-permute-done.21.refs_5_.refs_4_.refs_12_ = bf16[128,2048]{1,0:T(8,128)(2,1)S(1)} collective-permute-done((bf16[128,2048]{1,0:T(8,128)(2,1)}, bf16[128,2048]{1,0:T(8,128)(2,1)S(1)}, u32[]{:S(2)}, u32[]{:S(2)}) %collective-permute-start.21) | collective-permute-done | bytes 524320 | tf_op jit(solution)/shard_map/ppermute | solution.py:227
  107.4 1.6 %value_partial.6 = (bf16[256,256]{1,0:T(8,128)(2,1)S(1)}, f32[8,128]{1,0:T(8,128)S(1)}) custom-call(s32[1]{0:T(128)} %bitcast.x_at, f32[8,128]{1,0:T(8,128)S(1)} %get-tuple-element.85.token_in, bf16[256,512]{1,0:T(8,128)(2,1)S(1)} %get-tuple-element.86.refs_0_.refs_4_, bf16[256,512]{1,0:T(8,128)(2,1)S(1)} %collective-permute-done.17.refs_1_, ...), custom_call_target="tpu_custom_call" | custom-call | flops 1000 | bytes 1000 | tf_op jit(solution)/shard_map/value_partial/pallas_call | solution.py:131
  109.5 1.1 collective-permute-done.24.refs_3_
  111.3 2.1 %collective-permute-start.26 = (bf16[256,256]{1,0:T(8,128)(2,1)S(1)}, bf16[256,256]{1,0:T(8,128)(2,1)S(1)}, u32[]{:S(2)}, u32[]{:S(2)}) collective-permute-start(bf16[256,256]{1,0:T(8,128)(2,1)S(1)} %get-tuple-element.96), channel_id=1, source_target_pairs={{0,4},{1,5},{2,6},{3,7},{4,0},{5,1},{6,2},{7,3},{8,12},{9,13},{10,... | collective-permute-start | bytes 393224 | tf_op jit(solution)/shard_map/ppermute | solution.py:227
  113.4 1.4 dynamic-slice_bitcast_fusion.refs_4_.refs_2_.refs_10_
  114.8 1.0 copy-done.1
  115.9 1.6 %grad_value.6 = (bf16[256,256]{1,0:T(8,128)(2,1)S(1)}, f32[8,128]{1,0:T(8,128)S(1)}) custom-call(s32[1]{0:T(128)} %bitcast.x_at, f32[8,128]{1,0:T(8,128)S(1)} %get-tuple-element.91.token_in, bf16[256,512]{1,0:T(8,128)(2,1)S(1)} %get-tuple-element.86.refs_0_.refs_4_, bf16[256,512]{1,0:T(8,128)(2,1)S(1)} %collective-permute-done.17.refs_1_, ...), custom_call_target="tpu_custom_call" | custom-call | flops 1000 | bytes 1000 | tf_op jit(solution)/shard_map/grad_value/pallas_call | solution.py:131
  118.4 2.0 %collective-permute-start.28 = (bf16[256,256]{1,0:T(8,128)(2,1)S(1)}, bf16[256,256]{1,0:T(8,128)(2,1)S(1)}, u32[]{:S(2)}, u32[]{:S(2)}) collective-permute-start(bf16[256,256]{1,0:T(8,128)(2,1)S(1)} %get-tuple-element.100.refs_0_.refs_5_), channel_id=1, source_target_pairs={{0,4},{1,5},{2,6},{3,7},{4,0},{5,1},{6,2},{7,3},{8,12},{9,13},{10,... | collective-permute-start | bytes 393224 | tf_op jit(solution)/shard_map/ppermute | solution.py:227
  120.4 2.2 %collective-permute-done.27.refs_1_ = bf16[256,256]{1,0:T(8,128)(2,1)S(1)} collective-permute-done((bf16[256,256]{1,0:T(8,128)(2,1)S(1)}, bf16[256,256]{1,0:T(8,128)(2,1)S(1)}, u32[]{:S(2)}, u32[]{:S(2)}) %collective-permute-start.27) | collective-permute-done | bytes 131104 | tf_op jit(solution)/shard_map/ppermute | solution.py:227
  122.6 1.1 sum_partial.6
  123.6 3.2 %collective-permute-start.29 = (bf16[256,512]{1,0:T(8,128)(2,1)}, bf16[256,512]{1,0:T(8,128)(2,1)}, u32[]{:S(2)}, u32[]{:S(2)}) collective-permute-start(bf16[256,512]{1,0:T(8,128)(2,1)} %get-tuple-element.102), channel_id=1, source_target_pairs={{0,1},{1,2},{2,3},{3,0},{4,5},{5,6},{6,7},{7,4},{8,9},{9,10},{10,1... | collective-permute-start | bytes 786440 | tf_op jit(solution)/shard_map/ppermute | solution.py:227
  126.8 1.1 sum_partial.7
  128.6 3.3 %collective-permute-start.33 = (bf16[256,512]{1,0:T(8,128)(2,1)}, bf16[256,512]{1,0:T(8,128)(2,1)S(1)}, u32[]{:S(2)}, u32[]{:S(2)}) collective-permute-start(bf16[256,512]{1,0:T(8,128)(2,1)} %copy-done.15), channel_id=1, source_target_pairs={{0,1},{1,2},{2,3},{3,0},{4,5},{5,6},{6,7},{7,4},{8,9},{9,10},{10,1... | collective-permute-start | bytes 786440 | tf_op jit(solution)/shard_map/ppermute | solution.py:227
  131.8 2.0 %collective-permute-done.29.refs_5_ = bf16[256,512]{1,0:T(8,128)(2,1)} collective-permute-done((bf16[256,512]{1,0:T(8,128)(2,1)}, bf16[256,512]{1,0:T(8,128)(2,1)}, u32[]{:S(2)}, u32[]{:S(2)}) %collective-permute-start.29) | collective-permute-done | bytes 262176 | tf_op jit(solution)/shard_map/ppermute | solution.py:227
  133.9 1.3 sum_added.6
  135.2 3.8 %collective-permute-start.32 = (bf16[256,512]{1,0:T(8,128)(2,1)S(1)}, bf16[256,512]{1,0:T(8,128)(2,1)S(1)}, u32[]{:S(2)}, u32[]{:S(2)}) collective-permute-start(bf16[256,512]{1,0:T(8,128)(2,1)S(1)} %get-tuple-element.107), channel_id=1, source_target_pairs={{0,1},{1,2},{2,3},{3,0},{4,5},{5,6},{6,7},{7,4},{8,9},{9,10},{10,1... | collective-permute-start | bytes 786440 | tf_op jit(solution)/shard_map/ppermute | solution.py:227
  140.1 1.0 collective-permute-done.31.refs_2_
  143.5 3.4 %collective-permute-done.34.refs_8_ = bf16[256,512]{1,0:T(8,128)(2,1)S(1)} collective-permute-done((bf16[256,512]{1,0:T(8,128)(2,1)S(1)}, bf16[256,512]{1,0:T(8,128)(2,1)S(1)}, u32[]{:S(2)}, u32[]{:S(2)}) %collective-permute-start.34) | collective-permute-done | bytes 262176 | tf_op jit(solution)/shard_map/ppermute | solution.py:227
  147.0 1.2 copy-done.4
  148.2 0.9 copy-done.8
  149.2 0.9 copy-done.10
  150.1 0.9 copy-done.12
  151.1 1.9 %last_step.1 = (bf16[1,512,512]{2,1,0:T(8,128)(2,1)}, bf16[1,512,512]{2,1,0:T(8,128)(2,1)}, f32[8,128]{1,0:T(8,128)}) custom-call(s32[1]{0:T(128)} %bitcast.x_at, f32[8,128]{1,0:T(8,128)S(1)} %get-tuple-element.105.token_in, bf16[256,256]{1,0:T(8,128)(2,1)S(1)} %get-tuple-element.98.refs_0_, bf16[256,256]{1,0:T(8,128)(2,1)S(1)} %collective-permute-done.27.refs_1_, ...), custom_call_target="tpu_custom_call" | custom-call | flops 1000 | bytes 1000 | tf_op jit(solution)/shard_map/last_step/pallas_call | solution.py:131
  (109 shorter events, 15.5 us)
Async XLA Ops:
  7.2 36.6 %reduce-scatter.2.cloned.1.call-start = ((), (), s32[]{:S(2)}) async-start(), calls=%async_computation.1 | async-start | bytes 655360 | tf_op jit(solution)/shard_map/reduce_scatter | solution.py:345
  9.5 29.9 %collective-permute-start.3 = (bf16[256,2048]{1,0:T(8,128)(2,1)}, bf16[256,2048]{1,0:T(8,128)(2,1)S(1)}, u32[]{:S(2)}, u32[]{:S(2)}) collective-permute-start(bf16[256,2048]{1,0:T(8,128)(2,1)} %dynamic-slice_bitcast_fusion.2._), channel_id=1, source_target_pairs={{0,4},{1,5},{2,6},{3,7},{4,0},{5,1},{6,2},{7,3},{8,12},{9,13},{10,... | collective-permute-start | bytes 3145736 | tf_op jit(solution)/shard_map/ppermute | solution.py:227
  13.3 82.1 %all-gather.6.cloned.1.call-start = ((), (), s32[]{:S(2)}) async-start(), calls=%async_computation.3 | async-start | bytes 1310720 | tf_op jit(solution)/shard_map/all_gather | solution.py:342
  14.5 11.4 %collective-permute-start = (bf16[256,512]{1,0:T(8,128)(2,1)S(1)}, bf16[256,512]{1,0:T(8,128)(2,1)S(1)}, u32[]{:S(2)}, u32[]{:S(2)}) collective-permute-start(bf16[256,512]{1,0:T(8,128)(2,1)S(1)} %get-tuple-element.119.refs_0_.refs_6_), channel_id=1, source_target_pairs={{0,1},{1,2},{2,3},{3,0},{4,5},{5,6},{6,7},{7,4},{8,9},{9,10},{10,1... | collective-permute-start | bytes 786440 | tf_op jit(solution)/shard_map/ppermute | solution.py:227
  15.0 13.8 %collective-permute-start.5 = (bf16[256,512]{1,0:T(8,128)(2,1)S(1)}, bf16[256,512]{1,0:T(8,128)(2,1)S(1)}, u32[]{:S(2)}, u32[]{:S(2)}) collective-permute-start(bf16[256,512]{1,0:T(8,128)(2,1)S(1)} %get-tuple-element.118.refs_0_.refs_6_), channel_id=1, source_target_pairs={{0,3},{1,0},{2,1},{3,2},{4,7},{5,4},{6,5},{7,6},{8,11},{9,8},{10,9... | collective-permute-start | bytes 786440 | tf_op jit(solution)/shard_map/ppermute | solution.py:227
  16.6 22.9 %collective-permute-start.1 = (bf16[256,512]{1,0:T(8,128)(2,1)S(1)}, bf16[256,512]{1,0:T(8,128)(2,1)}, u32[]{:S(2)}, u32[]{:S(2)}) collective-permute-start(bf16[256,512]{1,0:T(8,128)(2,1)S(1)} %get-tuple-element.119.refs_0_.refs_6_), channel_id=1, source_target_pairs={{0,3},{1,0},{2,1},{3,2},{4,7},{5,4},{6,5},{7,6},{8,11},{9,8},{10,9... | collective-permute-start | bytes 786440 | tf_op jit(solution)/shard_map/ppermute | solution.py:227
  25.8 12.4 %copy-start.19 = (f32[16,512]{1,0:T(8,128)S(1)}, f32[16,512]{1,0:T(8,128)}, u32[]{:S(2)}) copy-start(f32[16,512]{1,0:T(8,128)} %param.12) | copy-start | bytes 98308
  25.8 13.0 %copy-start.21 = (f32[16,512]{1,0:T(8,128)S(1)}, f32[16,512]{1,0:T(8,128)}, u32[]{:S(2)}) copy-start(f32[16,512]{1,0:T(8,128)} %param.11) | copy-start | bytes 98308
  25.8 13.6 %collective-permute-start.2 = (bf16[256,512]{1,0:T(8,128)(2,1)S(1)}, bf16[256,512]{1,0:T(8,128)(2,1)}, u32[]{:S(2)}, u32[]{:S(2)}) collective-permute-start(bf16[256,512]{1,0:T(8,128)(2,1)S(1)} %collective-permute-done.refs_1_), channel_id=1, source_target_pairs={{0,1},{1,2},{2,3},{3,0},{4,5},{5,6},{6,7},{7,4},{8,9},{9,10},{10,1... | collective-permute-start | bytes 786440 | tf_op jit(solution)/shard_map/ppermute | solution.py:227
  28.3 13.3 %collective-permute-start.4 = (bf16[256,512]{1,0:T(8,128)(2,1)S(1)}, bf16[256,512]{1,0:T(8,128)(2,1)S(1)}, u32[]{:S(2)}, u32[]{:S(2)}) collective-permute-start(bf16[256,512]{1,0:T(8,128)(2,1)S(1)} %get-tuple-element.118.refs_0_.refs_6_), channel_id=1, source_target_pairs={{0,1},{1,2},{2,3},{3,0},{4,5},{5,6},{6,7},{7,4},{8,9},{9,10},{10,1... | collective-permute-start | bytes 786440 | tf_op jit(solution)/shard_map/ppermute | solution.py:227
  28.8 12.8 %collective-permute-start.6 = (bf16[256,512]{1,0:T(8,128)(2,1)S(1)}, bf16[256,512]{1,0:T(8,128)(2,1)}, u32[]{:S(2)}, u32[]{:S(2)}) collective-permute-start(bf16[256,512]{1,0:T(8,128)(2,1)S(1)} %collective-permute-done.5.refs_2_), channel_id=1, source_target_pairs={{0,3},{1,0},{2,1},{3,2},{4,7},{5,4},{6,5},{7,6},{8,11},{9,8},{10,9... | collective-permute-start | bytes 786440 | tf_op jit(solution)/shard_map/ppermute | solution.py:227
  38.2 18.2 %copy-start.2 = (bf16[4,256,256]{2,1,0:T(8,128)(2,1)S(1)}, bf16[4,256,256]{2,1,0:T(8,128)(2,1)}, u32[]{:S(2)}) copy-start(bf16[4,256,256]{2,1,0:T(8,128)(2,1)} %get-tuple-element.67.refs_6_) | copy-start | bytes 1572868
  38.2 18.2 %copy-start.3 = (f32[512,256]{1,0:T(8,128)S(1)}, f32[512,256]{1,0:T(8,128)}, u32[]{:S(2)}) copy-start(f32[512,256]{1,0:T(8,128)} %get-tuple-element.68.refs_7_) | copy-start | bytes 1572868
  39.5 0.7 copy-start.13
  41.6 0.7 copy-start.16
  45.3 1.7 %collective-permute-start.35 = (bf16[160,512]{1,0:T(8,128)(2,1)}, bf16[160,512]{1,0:T(8,128)(2,1)}, u32[]{:S(2)}, u32[]{:S(2)}) collective-permute-start(bf16[160,512]{1,0:T(8,128)(2,1)} %pad_maximum_fusion.1), channel_id=1, source_target_pairs={{0,8},{8,0},{16,24},{24,16},{32,40},{40,32},{48,56},{56,48},{64,72... | collective-permute-start | bytes 491528 | tf_op jit(solution)/shard_map/ppermute | solution.py:356
  49.7 97.3 %all-gather.4.cloned.1.call-start = ((), (), s32[]{:S(2)}) async-start(), calls=%async_computation.2 | async-start | bytes 1310720 | tf_op jit(solution)/shard_map/all_gather | solution.py:342
  49.7 6.6 %collective-permute-start.7 = (bf16[256,256]{1,0:T(8,128)(2,1)}, bf16[256,256]{1,0:T(8,128)(2,1)S(1)}, u32[]{:S(2)}, u32[]{:S(2)}) collective-permute-start(bf16[256,256]{1,0:T(8,128)(2,1)} %copy-done.16), channel_id=1, source_target_pairs={{0,4},{1,5},{2,6},{3,7},{4,0},{5,1},{6,2},{7,3},{8,12},{9,13},{10,... | collective-permute-start | bytes 393224 | tf_op jit(solution)/shard_map/ppermute | solution.py:227
  49.9 8.5 %collective-permute-start.8 = (bf16[256,256]{1,0:T(8,128)(2,1)S(1)}, bf16[256,256]{1,0:T(8,128)(2,1)S(1)}, u32[]{:S(2)}, u32[]{:S(2)}) collective-permute-start(bf16[256,256]{1,0:T(8,128)(2,1)S(1)} %get-tuple-element.70), channel_id=1, source_target_pairs={{0,4},{1,5},{2,6},{3,7},{4,0},{5,1},{6,2},{7,3},{8,12},{9,13},{10,... | collective-permute-start | bytes 393224 | tf_op jit(solution)/shard_map/ppermute | solution.py:227
  58.1 6.5 %collective-permute-start.9 = (bf16[256,256]{1,0:T(8,128)(2,1)S(1)}, bf16[256,256]{1,0:T(8,128)(2,1)S(1)}, u32[]{:S(2)}, u32[]{:S(2)}) collective-permute-start(bf16[256,256]{1,0:T(8,128)(2,1)S(1)} %get-tuple-element.72.refs_0_), channel_id=1, source_target_pairs={{0,4},{1,5},{2,6},{3,7},{4,0},{5,1},{6,2},{7,3},{8,12},{9,13},{10,... | collective-permute-start | bytes 393224 | tf_op jit(solution)/shard_map/ppermute | solution.py:227
  60.1 11.7 %collective-permute-start.10 = (bf16[256,256]{1,0:T(8,128)(2,1)S(1)}, bf16[256,256]{1,0:T(8,128)(2,1)S(1)}, u32[]{:S(2)}, u32[]{:S(2)}) collective-permute-start(bf16[256,256]{1,0:T(8,128)(2,1)S(1)} %get-tuple-element.74.refs_0_), channel_id=1, source_target_pairs={{0,4},{1,5},{2,6},{3,7},{4,0},{5,1},{6,2},{7,3},{8,12},{9,13},{10,... | collective-permute-start | bytes 393224 | tf_op jit(solution)/shard_map/ppermute | solution.py:227
  65.1 8.1 %collective-permute-start.11 = (bf16[256,512]{1,0:T(8,128)(2,1)S(1)}, bf16[256,512]{1,0:T(8,128)(2,1)S(1)}, u32[]{:S(2)}, u32[]{:S(2)}) collective-permute-start(bf16[256,512]{1,0:T(8,128)(2,1)S(1)} %get-tuple-element.76), channel_id=1, source_target_pairs={{0,1},{1,2},{2,3},{3,0},{4,5},{5,6},{6,7},{7,4},{8,9},{9,10},{10,1... | collective-permute-start | bytes 786440 | tf_op jit(solution)/shard_map/ppermute | solution.py:227
  72.2 10.4 %collective-permute-start.12 = (bf16[256,512]{1,0:T(8,128)(2,1)S(1)}, bf16[256,512]{1,0:T(8,128)(2,1)S(1)}, u32[]{:S(2)}, u32[]{:S(2)}) collective-permute-start(bf16[256,512]{1,0:T(8,128)(2,1)S(1)} %get-tuple-element.78), channel_id=1, source_target_pairs={{0,3},{1,0},{2,1},{3,2},{4,7},{5,4},{6,5},{7,6},{8,11},{9,8},{10,9... | collective-permute-start | bytes 786440 | tf_op jit(solution)/shard_map/ppermute | solution.py:227
  72.3 15.6 %collective-permute-start.13 = (bf16[256,512]{1,0:T(8,128)(2,1)S(1)}, bf16[256,512]{1,0:T(8,128)(2,1)S(1)}, u32[]{:S(2)}, u32[]{:S(2)}) collective-permute-start(bf16[256,512]{1,0:T(8,128)(2,1)S(1)} %get-tuple-element.80), channel_id=1, source_target_pairs={{0,3},{1,0},{2,1},{3,2},{4,7},{5,4},{6,5},{7,6},{8,11},{9,8},{10,9... | collective-permute-start | bytes 786440 | tf_op jit(solution)/shard_map/ppermute | solution.py:227
  73.5 14.3 %collective-permute-start.14 = (bf16[256,512]{1,0:T(8,128)(2,1)S(1)}, bf16[256,512]{1,0:T(8,128)(2,1)S(1)}, u32[]{:S(2)}, u32[]{:S(2)}) collective-permute-start(bf16[256,512]{1,0:T(8,128)(2,1)S(1)} %get-tuple-element.81), channel_id=1, source_target_pairs={{0,1},{1,2},{2,3},{3,0},{4,5},{5,6},{6,7},{7,4},{8,9},{9,10},{10,1... | collective-permute-start | bytes 786440 | tf_op jit(solution)/shard_map/ppermute | solution.py:227
  76.0 14.4 %collective-permute-start.15 = (bf16[256,512]{1,0:T(8,128)(2,1)S(1)}, bf16[256,512]{1,0:T(8,128)(2,1)S(1)}, u32[]{:S(2)}, u32[]{:S(2)}) collective-permute-start(bf16[256,512]{1,0:T(8,128)(2,1)S(1)} %get-tuple-element.83), channel_id=1, source_target_pairs={{0,1},{1,2},{2,3},{3,0},{4,5},{5,6},{6,7},{7,4},{8,9},{9,10},{10,1... | collective-permute-start | bytes 786440 | tf_op jit(solution)/shard_map/ppermute | solution.py:227
  82.9 10.2 %collective-permute-start.16 = (bf16[256,512]{1,0:T(8,128)(2,1)S(1)}, bf16[256,512]{1,0:T(8,128)(2,1)S(1)}, u32[]{:S(2)}, u32[]{:S(2)}) collective-permute-start(bf16[256,512]{1,0:T(8,128)(2,1)S(1)} %get-tuple-element.84), channel_id=1, source_target_pairs={{0,3},{1,0},{2,1},{3,2},{4,7},{5,4},{6,5},{7,6},{8,11},{9,8},{10,9... | collective-permute-start | bytes 786440 | tf_op jit(solution)/shard_map/ppermute | solution.py:227
  84.9 19.0 %collective-permute-start.20 = (bf16[128,2048]{1,0:T(8,128)(2,1)}, bf16[128,2048]{1,0:T(8,128)(2,1)S(1)}, u32[]{:S(2)}, u32[]{:S(2)}) collective-permute-start(bf16[128,2048]{1,0:T(8,128)(2,1)} %dynamic-slice_bitcast_fusion.4), channel_id=1, source_target_pairs={{0,4},{1,5},{2,6},{3,7},{4,0},{5,1},{6,2},{7,3},{8,12},{9,13},{10,... | collective-permute-start | bytes 1572872 | tf_op jit(solution)/shard_map/ppermute | solution.py:227
  88.2 10.3 %collective-permute-start.17 = (bf16[256,512]{1,0:T(8,128)(2,1)S(1)}, bf16[256,512]{1,0:T(8,128)(2,1)S(1)}, u32[]{:S(2)}, u32[]{:S(2)}) collective-permute-start(bf16[256,512]{1,0:T(8,128)(2,1)S(1)} %get-tuple-element.86.refs_0_.refs_4_), channel_id=1, source_target_pairs={{0,1},{1,2},{2,3},{3,0},{4,5},{5,6},{6,7},{7,4},{8,9},{9,10},{10,1... | collective-permute-start | bytes 786440 | tf_op jit(solution)/shard_map/ppermute | solution.py:227
  88.6 13.2 %collective-permute-start.18 = (bf16[256,512]{1,0:T(8,128)(2,1)S(1)}, bf16[256,512]{1,0:T(8,128)(2,1)}, u32[]{:S(2)}, u32[]{:S(2)}) collective-permute-start(bf16[256,512]{1,0:T(8,128)(2,1)S(1)} %get-tuple-element.86.refs_0_.refs_4_), channel_id=1, source_target_pairs={{0,3},{1,0},{2,1},{3,2},{4,7},{5,4},{6,5},{7,6},{8,11},{9,8},{10,9... | collective-permute-start | bytes 786440 | tf_op jit(solution)/shard_map/ppermute | solution.py:227
  95.4 12.0 %collective-permute-start.21 = (bf16[128,2048]{1,0:T(8,128)(2,1)}, bf16[128,2048]{1,0:T(8,128)(2,1)S(1)}, u32[]{:S(2)}, u32[]{:S(2)}) collective-permute-start(bf16[128,2048]{1,0:T(8,128)(2,1)} %dynamic-slice_bitcast_fusion.3), channel_id=1, source_target_pairs={{0,4},{1,5},{2,6},{3,7},{4,0},{5,1},{6,2},{7,3},{8,12},{9,13},{10,... | collective-permute-start | bytes 1572872 | tf_op jit(solution)/shard_map/ppermute | solution.py:227
  95.4 7.6 %collective-permute-start.23 = (bf16[256,512]{1,0:T(8,128)(2,1)S(1)}, bf16[256,512]{1,0:T(8,128)(2,1)S(1)}, u32[]{:S(2)}, u32[]{:S(2)}) collective-permute-start(bf16[256,512]{1,0:T(8,128)(2,1)S(1)} %get-tuple-element.90.refs_0_.refs_9_), channel_id=1, source_target_pairs={{0,3},{1,0},{2,1},{3,2},{4,7},{5,4},{6,5},{7,6},{8,11},{9,8},{10,9... | collective-permute-start | bytes 786440 | tf_op jit(solution)/shard_map/ppermute | solution.py:227
  97.7 13.6 %copy-start.17 = (f32[128,512]{1,0:T(8,128)}, f32[128,512]{1,0:T(8,128)S(1)}, u32[]{:S(2)}) copy-start(f32[128,512]{1,0:T(8,128)S(1)} %convert_reduce_fusion) | copy-start | bytes 786436
  97.7 17.1 %copy-start = (bf16[4,256,256]{2,1,0:T(8,128)(2,1)S(1)}, bf16[4,256,256]{2,1,0:T(8,128)(2,1)}, u32[]{:S(2)}) copy-start(bf16[4,256,256]{2,1,0:T(8,128)(2,1)} %get-tuple-element.93.refs_6_) | copy-start | bytes 1572868
  98.6 7.2 %collective-permute-start.19 = (bf16[256,512]{1,0:T(8,128)(2,1)S(1)}, bf16[256,512]{1,0:T(8,128)(2,1)S(1)}, u32[]{:S(2)}, u32[]{:S(2)}) collective-permute-start(bf16[256,512]{1,0:T(8,128)(2,1)S(1)} %collective-permute-done.17.refs_1_), channel_id=1, source_target_pairs={{0,1},{1,2},{2,3},{3,0},{4,5},{5,6},{6,7},{7,4},{8,9},{9,10},{10,1... | collective-permute-start | bytes 786440 | tf_op jit(solution)/shard_map/ppermute | solution.py:227
  101.8 7.7 %collective-permute-start.22 = (bf16[256,512]{1,0:T(8,128)(2,1)S(1)}, bf16[256,512]{1,0:T(8,128)(2,1)S(1)}, u32[]{:S(2)}, u32[]{:S(2)}) collective-permute-start(bf16[256,512]{1,0:T(8,128)(2,1)S(1)} %get-tuple-element.90.refs_0_.refs_9_), channel_id=1, source_target_pairs={{0,1},{1,2},{2,3},{3,0},{4,5},{5,6},{6,7},{7,4},{8,9},{9,10},{10,1... | collective-permute-start | bytes 786440 | tf_op jit(solution)/shard_map/ppermute | solution.py:227
  103.0 8.3 %copy-start.5 = (bf16[256,512]{1,0:T(8,128)(2,1)}, bf16[256,512]{1,0:T(8,128)(2,1)S(1)}, u32[]{:S(2)}) copy-start(bf16[256,512]{1,0:T(8,128)(2,1)S(1)} %collective-permute-done.23.refs_2_) | copy-start | bytes 786436
  103.0 7.6 %collective-permute-start.24 = (bf16[256,512]{1,0:T(8,128)(2,1)S(1)}, bf16[256,512]{1,0:T(8,128)(2,1)S(1)}, u32[]{:S(2)}, u32[]{:S(2)}) collective-permute-start(bf16[256,512]{1,0:T(8,128)(2,1)S(1)} %collective-permute-done.23.refs_2_), channel_id=1, source_target_pairs={{0,3},{1,0},{2,1},{3,2},{4,7},{5,4},{6,5},{7,6},{8,11},{9,8},{10,9... | collective-permute-start | bytes 786440 | tf_op jit(solution)/shard_map/ppermute | solution.py:227
  109.1 5.7 %collective-permute-start.25 = (bf16[256,256]{1,0:T(8,128)(2,1)S(1)}, bf16[256,256]{1,0:T(8,128)(2,1)S(1)}, u32[]{:S(2)}, u32[]{:S(2)}) collective-permute-start(bf16[256,256]{1,0:T(8,128)(2,1)S(1)} %get-tuple-element.92), channel_id=1, source_target_pairs={{0,4},{1,5},{2,6},{3,7},{4,0},{5,1},{6,2},{7,3},{8,12},{9,13},{10,... | collective-permute-start | bytes 393224 | tf_op jit(solution)/shard_map/ppermute | solution.py:227
  111.3 6.4 %collective-permute-start.26 = (bf16[256,256]{1,0:T(8,128)(2,1)S(1)}, bf16[256,256]{1,0:T(8,128)(2,1)S(1)}, u32[]{:S(2)}, u32[]{:S(2)}) collective-permute-start(bf16[256,256]{1,0:T(8,128)(2,1)S(1)} %get-tuple-element.96), channel_id=1, source_target_pairs={{0,4},{1,5},{2,6},{3,7},{4,0},{5,1},{6,2},{7,3},{8,12},{9,13},{10,... | collective-permute-start | bytes 393224 | tf_op jit(solution)/shard_map/ppermute | solution.py:227
  113.4 4.3 %copy-start.6 = (bf16[256,512]{1,0:T(8,128)(2,1)S(1)}, bf16[256,512]{1,0:T(8,128)(2,1)}, u32[]{:S(2)}) copy-start(bf16[256,512]{1,0:T(8,128)(2,1)} %copy-done.5) | copy-start | bytes 786436
  114.8 1.1 copy-start.1
  117.5 5.1 %collective-permute-start.27 = (bf16[256,256]{1,0:T(8,128)(2,1)S(1)}, bf16[256,256]{1,0:T(8,128)(2,1)S(1)}, u32[]{:S(2)}, u32[]{:S(2)}) collective-permute-start(bf16[256,256]{1,0:T(8,128)(2,1)S(1)} %get-tuple-element.98.refs_0_), channel_id=1, source_target_pairs={{0,4},{1,5},{2,6},{3,7},{4,0},{5,1},{6,2},{7,3},{8,12},{9,13},{10,... | collective-permute-start | bytes 393224 | tf_op jit(solution)/shard_map/ppermute | solution.py:227
  118.4 8.4 %collective-permute-start.28 = (bf16[256,256]{1,0:T(8,128)(2,1)S(1)}, bf16[256,256]{1,0:T(8,128)(2,1)S(1)}, u32[]{:S(2)}, u32[]{:S(2)}) collective-permute-start(bf16[256,256]{1,0:T(8,128)(2,1)S(1)} %get-tuple-element.100.refs_0_.refs_5_), channel_id=1, source_target_pairs={{0,4},{1,5},{2,6},{3,7},{4,0},{5,1},{6,2},{7,3},{8,12},{9,13},{10,... | collective-permute-start | bytes 393224 | tf_op jit(solution)/shard_map/ppermute | solution.py:227
  123.6 3.2 %copy-start.14 = (bf16[256,512]{1,0:T(8,128)(2,1)}, bf16[256,512]{1,0:T(8,128)(2,1)S(1)}, u32[]{:S(2)}) copy-start(bf16[256,512]{1,0:T(8,128)(2,1)S(1)} %get-tuple-element.106) | copy-start | bytes 786436
  123.6 15.8 %copy-start.20 = (f32[16,512]{1,0:T(8,128)S(1)}, f32[16,512]{1,0:T(8,128)}, u32[]{:S(2)}) copy-start(f32[16,512]{1,0:T(8,128)} %param.12) | copy-start | bytes 98308
  123.6 15.8 %copy-start.22 = (f32[16,512]{1,0:T(8,128)S(1)}, f32[16,512]{1,0:T(8,128)}, u32[]{:S(2)}) copy-start(f32[16,512]{1,0:T(8,128)} %param.11) | copy-start | bytes 98308
  123.6 10.2 %collective-permute-start.29 = (bf16[256,512]{1,0:T(8,128)(2,1)}, bf16[256,512]{1,0:T(8,128)(2,1)}, u32[]{:S(2)}, u32[]{:S(2)}) collective-permute-start(bf16[256,512]{1,0:T(8,128)(2,1)} %get-tuple-element.102), channel_id=1, source_target_pairs={{0,1},{1,2},{2,3},{3,0},{4,5},{5,6},{6,7},{7,4},{8,9},{9,10},{10,1... | collective-permute-start | bytes 786440 | tf_op jit(solution)/shard_map/ppermute | solution.py:227
  127.9 0.7 copy-start.15
  128.6 10.4 %collective-permute-start.30 = (bf16[256,512]{1,0:T(8,128)(2,1)}, bf16[256,512]{1,0:T(8,128)(2,1)S(1)}, u32[]{:S(2)}, u32[]{:S(2)}) collective-permute-start(bf16[256,512]{1,0:T(8,128)(2,1)} %get-tuple-element.104), channel_id=1, source_target_pairs={{0,3},{1,0},{2,1},{3,2},{4,7},{5,4},{6,5},{7,6},{8,11},{9,8},{10,9... | collective-permute-start | bytes 786440 | tf_op jit(solution)/shard_map/ppermute | solution.py:227
  128.6 10.8 %copy-start.18 = (f32[128,512]{1,0:T(8,128)S(1)}, f32[128,512]{1,0:T(8,128)}, u32[]{:S(2)}) copy-start(f32[128,512]{1,0:T(8,128)} %copy-done.17) | copy-start | bytes 786436
  128.6 12.6 %collective-permute-start.31 = (bf16[256,512]{1,0:T(8,128)(2,1)}, bf16[256,512]{1,0:T(8,128)(2,1)S(1)}, u32[]{:S(2)}, u32[]{:S(2)}) collective-permute-start(bf16[256,512]{1,0:T(8,128)(2,1)} %copy-done.14), channel_id=1, source_target_pairs={{0,3},{1,0},{2,1},{3,2},{4,7},{5,4},{6,5},{7,6},{8,11},{9,8},{10,9... | collective-permute-start | bytes 786440 | tf_op jit(solution)/shard_map/ppermute | solution.py:227
  128.6 13.3 %collective-permute-start.33 = (bf16[256,512]{1,0:T(8,128)(2,1)}, bf16[256,512]{1,0:T(8,128)(2,1)S(1)}, u32[]{:S(2)}, u32[]{:S(2)}) collective-permute-start(bf16[256,512]{1,0:T(8,128)(2,1)} %copy-done.15), channel_id=1, source_target_pairs={{0,1},{1,2},{2,3},{3,0},{4,5},{5,6},{6,7},{7,4},{8,9},{9,10},{10,1... | collective-permute-start | bytes 786440 | tf_op jit(solution)/shard_map/ppermute | solution.py:227
  135.2 7.7 %collective-permute-start.32 = (bf16[256,512]{1,0:T(8,128)(2,1)S(1)}, bf16[256,512]{1,0:T(8,128)(2,1)S(1)}, u32[]{:S(2)}, u32[]{:S(2)}) collective-permute-start(bf16[256,512]{1,0:T(8,128)(2,1)S(1)} %get-tuple-element.107), channel_id=1, source_target_pairs={{0,1},{1,2},{2,3},{3,0},{4,5},{5,6},{6,7},{7,4},{8,9},{9,10},{10,1... | collective-permute-start | bytes 786440 | tf_op jit(solution)/shard_map/ppermute | solution.py:227
  139.3 7.7 %collective-permute-start.34 = (bf16[256,512]{1,0:T(8,128)(2,1)S(1)}, bf16[256,512]{1,0:T(8,128)(2,1)S(1)}, u32[]{:S(2)}, u32[]{:S(2)}) collective-permute-start(bf16[256,512]{1,0:T(8,128)(2,1)S(1)} %get-tuple-element.109), channel_id=1, source_target_pairs={{0,3},{1,0},{2,1},{3,2},{4,7},{5,4},{6,5},{7,6},{8,11},{9,8},{10,9... | collective-permute-start | bytes 786440 | tf_op jit(solution)/shard_map/ppermute | solution.py:227
  141.1 0.7 copy-start.7
  141.9 0.7 copy-start.9
  142.8 0.7 copy-start.11
  147.0 1.2 copy-start.4
  148.2 0.9 copy-start.8
  149.2 0.9 copy-start.10
  150.1 0.9 copy-start.12
Sparse Core Ops, SparseCore 0:
  13.5 22.8 reduce-scatter.1
  49.8 36.9 all-gather.5
  98.7 29.8 all-gather.3
where the time goes:
time: 160 us; the launch traced here: 159 us
  starting transfers between devices  42 us (26%)
  waiting for transfers between devices  38.1 us (24%)
  Pallas kernels  34.5 us (22%)
  local copies, waits for them, and re-layouts  22.6 us (14%)
  between operations  14.2 us (9%)
  other arithmetic  8.08 us (5%)
    ppermute x35, starting transfers between devices, send(): return lax.ppermute(value, 'fsdp', perm)  41.9 us
    ppermute x35, waiting for transfers between devices, send(): return lax.ppermute(value, 'fsdp', perm)  36.4 us
    pallas_call x19, Pallas kernels, ordered(): pl.pallas_call(kernel, in_specs=[SMEM] + [VMEM] * (1 + len(operands)), ou...  18.8 us
    pallas_call x2, Pallas kernels, attention_matrices(): pl.pallas_call(attention_kernel, grid=(KVH,), in_specs=[pl.BlockSpec(memo...  15.7 us
    unnamed x46, local copies, waits for them, and re-layouts  9.27 us
    squeeze x3, local copies, waits for them, and re-layouts, columns(): return lax.dynamic_slice(rows, start, (1, 1, length, half_width))[0, 0]  4.97 us
    squeeze x2, local copies, waits for them, and re-layouts, swap_rows(): return send(away[0, 0], Z_SWAP)  3.78 us
  transfers between devices with their start and end apart: 39, of which 18 were waited for; matrix products, arithmetic and copies ran while one was open for 9% of the time, Pallas kernels for 20%

commit v1 on v0

--- a/solution.py
+++ b/solution.py
@@ -298,6 +298,9 @@
             (opp, plain), token = ordered(body, "sum_partial", x_id, token, operands[c], [piece, piece])
             opp_in[c] = send(opp, there[c])
             plain_in[c] = send(plain, back[c])
+        if step + 1 < STEPS:
+            next_mine = columns(gated(inputs, token), step + 1, z_id)
+            next_other = [swap_rows(gated(inputs, token), step + 1, 0)]
         for c in chunks:
             body = functools.partial(add_body, sides[c])
             (added,), token = ordered(body, "sum_added", x_id, token, [*operands[c], opp_in[c]], [piece])
@@ -305,8 +308,7 @@
         if step + 1 == STEPS:
             break
         outer.send(token)
-        next_mine = columns(gated(inputs, token), step + 1, z_id)
-        next_other = [swap_rows(gated(inputs, token), step + 1, 0)]
+        next_other.append(swap_rows(gated(inputs, token), step + 1, 1))
         for c in chunks:
             (w_now[c],), token = ordered(
                 functools.partial(step_body, rate),
@@ -317,7 +319,6 @@
                 [piece],
             )
             gathered[c] = gather_x(sides[c], w_now[c])
-        next_other.append(swap_rows(gated(inputs, token), step + 1, 1))
         mine, other = next_mine, next_other
     args = []
     for c in chunks:
@@ -349,7 +350,7 @@
         axis_index_groups=along_y,
         tiled=True,
     )
-    owns = jnp.concatenate([anchor.astype(BF), momentum.astype(BF)], axis=0)
+    owns = jnp.concatenate([anchor, momentum], axis=0).astype(BF)
     token = yield
     rows = sums.shape[0]
     here = gated(jnp.concatenate([sums, owns], axis=0), token)

time: 160 us -> 160 us (level)
  waiting for transfers between devices: 38.1 us -> 32.4 us
  starting transfers between devices: 42 us -> 45.9 us
    ppermute x35, waiting for transfers between devices: 36.4 us -> 30.7 us  [send(): return lax.ppermute(value, 'fsdp', perm)]
    ppermute x35, starting transfers between devices: 41.9 us -> 45.8 us  [send(): return lax.ppermute(value, 'fsdp', perm)]
    unnamed x46, local copies, waits for them, and re-layouts: 9.27 us -> 10.9 us
  transfers between devices with their start and end apart: 39 -> 39, of which waited for: 18 -> 16; matrix products, arithmetic and copies ran while one was open for 9% -> 9% of each run, Pallas kernels for 20% -> 20%
where the time goes in v1:
time: 160 us; the launch traced here: 159 us
  starting transfers between devices  45.9 us (29%)
  Pallas kernels  34.5 us (22%)
  waiting for transfers between devices  32.4 us (20%)
  local copies, waits for them, and re-layouts  24.2 us (15%)
  between operations  14.2 us (9%)
  other arithmetic  8.09 us (5%)
    ppermute x35, starting transfers between devices, send(): return lax.ppermute(value, 'fsdp', perm)  45.8 us
    ppermute x35, waiting for transfers between devices, send(): return lax.ppermute(value, 'fsdp', perm)  30.7 us
    pallas_call x19, Pallas kernels, ordered(): pl.pallas_call(kernel, in_specs=[SMEM] + [VMEM] * (1 + len(operands)), ou...  18.8 us
    pallas_call x2, Pallas kernels, attention_matrices(): pl.pallas_call(attention_kernel, grid=(KVH,), in_specs=[pl.BlockSpec(memo...  15.7 us
    unnamed x46, local copies, waits for them, and re-layouts  10.9 us
    squeeze x3, local copies, waits for them, and re-layouts, columns(): return lax.dynamic_slice(rows, start, (1, 1, length, half_width))[0, 0]  4.93 us
    squeeze x2, local copies, waits for them, and re-layouts, swap_rows(): return send(away[0, 0], Z_SWAP)  3.77 us
  transfers between devices with their start and end apart: 39, of which 16 were waited for; matrix products, arithmetic and copies ran while one was open for 9% of the time, Pallas kernels for 20%

profile of v1, /device:TPU:94, one launch (start us, length us, event | category | flops | bytes accessed | tf_op | source)
XLA Modules:
  0.0 159.3 jit_solution(11008638003080228372)
XLA Ops:
  7.2 2.3 %dynamic-slice_bitcast_fusion.2._ = bf16[256,2048]{1,0:T(8,128)(2,1)} fusion(bf16[1,2,256,4096]{3,2,1,0:T(8,128)(2,1)} %x_ref.3, s32[]{:T(128)S(6)} %select_n.46), kind=kLoop, calls=%fused_computation.3 | loop fusion | bytes 2097156 | tf_op jit(solution)/shard_map/squeeze | solution.py:260
  9.5 1.9 %collective-permute-start.3 = (bf16[256,2048]{1,0:T(8,128)(2,1)}, bf16[256,2048]{1,0:T(8,128)(2,1)S(1)}, u32[]{:S(2)}, u32[]{:S(2)}) collective-permute-start(bf16[256,2048]{1,0:T(8,128)(2,1)} %dynamic-slice_bitcast_fusion.2._), channel_id=1, source_target_pairs={{0,4},{1,5},{2,6},{3,7},{4,0},{5,1},{6,2},{7,3},{8,12},{9,13},{10,... | collective-permute-start | bytes 3145736 | tf_op jit(solution)/shard_map/ppermute | solution.py:227
  11.5 1.9 %copy.12 = bf16[4,4,32,512]{3,2,1,0:T(8,128)(2,1)} copy(bf16[4,4,32,512]{3,2,0,1:T(8,128)(2,1)} %bitcast.52) | data formatting | bytes 1048576 | tf_op jit(solution)/shard_map/transpose | solution.py:345
  13.4 1.1 slice_bitcast_fusion
  15.0 1.5 collective-permute-start.5
  16.6 0.8 collective-permute-start.1
  18.0 7.8 %attention_matrices.2 = (bf16[4,256,256]{2,1,0:T(8,128)(2,1)}, f32[512,256]{1,0:T(8,128)}, f32[8,128]{1,0:T(8,128)}) custom-call(bf16[256,2048]{1,0:T(8,128)(2,1)} %dynamic-slice_bitcast_fusion.2._, f32[8,128]{1,0:T(8,128)} %broadcast_in_dim.3.t_in, bf16[1,2,256,4096]{3,2,1,0:T(8,128)(2,1)} %q_ref.3, bf16[1,2,256,512]{3,2,1,0:T(8,128)(2,1)} %k_ref.3, ...), custom_call_target="tpu_custom_call" | custom-call | flops 1000 | bytes 1000 | tf_op jit(solution)/shard_map/attention_matrices/pallas_call | solution.py:90
  25.8 2.5 %collective-permute-start.2 = (bf16[256,512]{1,0:T(8,128)(2,1)S(1)}, bf16[256,512]{1,0:T(8,128)(2,1)}, u32[]{:S(2)}, u32[]{:S(2)}) collective-permute-start(bf16[256,512]{1,0:T(8,128)(2,1)S(1)} %collective-permute-done.refs_1_), channel_id=1, source_target_pairs={{0,1},{1,2},{2,3},{3,0},{4,5},{5,6},{6,7},{7,4},{8,9},{9,10},{10,1... | collective-permute-start | bytes 786440 | tf_op jit(solution)/shard_map/ppermute | solution.py:227
  28.8 1.5 collective-permute-start.6
  30.4 7.8 %attention_matrices.3 = (bf16[4,256,256]{2,1,0:T(8,128)(2,1)}, f32[512,256]{1,0:T(8,128)}, f32[8,128]{1,0:T(8,128)}) custom-call(bf16[256,2048]{1,0:T(8,128)(2,1)} %dynamic-slice_bitcast_fusion.2._, f32[8,128]{1,0:T(8,128)} %get-tuple-element.59.t_in, bf16[1,2,256,4096]{3,2,1,0:T(8,128)(2,1)} %q_ref.3, bf16[1,2,256,512]{3,2,1,0:T(8,128)(2,1)} %k_ref.3, ...), custom_call_target="tpu_custom_call" | custom-call | flops 1000 | bytes 1000 | tf_op jit(solution)/shard_map/attention_matrices/pallas_call | solution.py:90
  40.1 1.5 value_partial.4
  42.3 1.4 value_partial.5
  43.7 1.6 %pad_maximum_fusion.1 = bf16[160,512]{1,0:T(8,128)(2,1)} fusion(bf16[16,512]{1,0:T(8,128)(2,1)} %convert.17, bf16[16,512]{1,0:T(8,128)(2,1)} %convert.16, bf16[128,512]{1,0:T(8,128)(2,1)} %reduce-scatter.2.cloned.1.call-done), kind=kLoop, calls=%fused_computation.19 | loop fusion | flops 491520 | bytes 327680 | tf_op jit(solution)/shard_map/concatenate | solution.py:356
  45.4 1.7 %collective-permute-done.35 = bf16[160,512]{1,0:T(8,128)(2,1)} collective-permute-done((bf16[160,512]{1,0:T(8,128)(2,1)}, bf16[160,512]{1,0:T(8,128)(2,1)}, u32[]{:S(2)}, u32[]{:S(2)}) %collective-permute-start.35) | collective-permute-done | bytes 163872 | tf_op jit(solution)/shard_map/ppermute | solution.py:357
  47.1 1.0 add_convert_fusion
  48.1 0.8 broadcast_select_fusion.1
  48.9 0.8 maximum_maximum_fusion
  49.9 1.9 %collective-permute-start.8 = (bf16[256,256]{1,0:T(8,128)(2,1)S(1)}, bf16[256,256]{1,0:T(8,128)(2,1)S(1)}, u32[]{:S(2)}, u32[]{:S(2)}) collective-permute-start(bf16[256,256]{1,0:T(8,128)(2,1)S(1)} %get-tuple-element.70), channel_id=1, source_target_pairs={{0,4},{1,5},{2,6},{3,7},{4,0},{5,1},{6,2},{7,3},{8,12},{9,13},{10,... | collective-permute-start | bytes 393224 | tf_op jit(solution)/shard_map/ppermute | solution.py:227
  51.9 1.3 dynamic-slice_bitcast_fusion.1.refs_4_.refs_2_
  53.2 3.2 %collective-permute-done.7.refs_5_ = bf16[256,256]{1,0:T(8,128)(2,1)S(1)} collective-permute-done((bf16[256,256]{1,0:T(8,128)(2,1)}, bf16[256,256]{1,0:T(8,128)(2,1)S(1)}, u32[]{:S(2)}, u32[]{:S(2)}) %collective-permute-start.7) | collective-permute-done | bytes 131104 | tf_op jit(solution)/shard_map/ppermute | solution.py:227
  56.4 1.7 %grad_value.4 = (bf16[256,256]{1,0:T(8,128)(2,1)S(1)}, f32[8,128]{1,0:T(8,128)S(1)}) custom-call(s32[1]{0:T(128)} %bitcast.x_at, f32[8,128]{1,0:T(8,128)S(1)} %get-tuple-element.64.token_in, bf16[256,512]{1,0:T(8,128)(2,1)S(1)} %get-tuple-element.119.refs_0_.refs_6_, bf16[256,512]{1,0:T(8,128)(2,1)S(1)} %collective-permute-done.refs_1_, ...), custom_call_target="tpu_custom_call" | custom-call | flops 1000 | bytes 1000 | tf_op jit(solution)/shard_map/grad_value/pallas_call | solution.py:131
  58.5 1.6 %grad_value.5 = (bf16[256,256]{1,0:T(8,128)(2,1)S(1)}, f32[8,128]{1,0:T(8,128)S(1)}) custom-call(s32[1]{0:T(128)} %bitcast.x_at, f32[8,128]{1,0:T(8,128)S(1)} %get-tuple-element.69.token_in, bf16[256,512]{1,0:T(8,128)(2,1)S(1)} %get-tuple-element.118.refs_0_.refs_6_, bf16[256,512]{1,0:T(8,128)(2,1)S(1)} %collective-permute-done.4.refs_1_, ...), custom_call_target="tpu_custom_call" | custom-call | flops 1000 | bytes 1000 | tf_op jit(solution)/shard_map/grad_value/pallas_call | solution.py:131
  60.1 2.0 %collective-permute-start.10 = (bf16[256,256]{1,0:T(8,128)(2,1)S(1)}, bf16[256,256]{1,0:T(8,128)(2,1)S(1)}, u32[]{:S(2)}, u32[]{:S(2)}) collective-permute-start(bf16[256,256]{1,0:T(8,128)(2,1)S(1)} %get-tuple-element.74.refs_0_), channel_id=1, source_target_pairs={{0,4},{1,5},{2,6},{3,7},{4,0},{5,1},{6,2},{7,3},{8,12},{9,13},{10,... | collective-permute-start | bytes 393224 | tf_op jit(solution)/shard_map/ppermute | solution.py:227
  62.1 2.5 %collective-permute-done.9.refs_1_ = bf16[256,256]{1,0:T(8,128)(2,1)S(1)} collective-permute-done((bf16[256,256]{1,0:T(8,128)(2,1)S(1)}, bf16[256,256]{1,0:T(8,128)(2,1)S(1)}, u32[]{:S(2)}, u32[]{:S(2)}) %collective-permute-start.9) | collective-permute-done | bytes 131104 | tf_op jit(solution)/shard_map/ppermute | solution.py:227
  65.1 1.9 %collective-permute-start.11 = (bf16[256,512]{1,0:T(8,128)(2,1)S(1)}, bf16[256,512]{1,0:T(8,128)(2,1)S(1)}, u32[]{:S(2)}, u32[]{:S(2)}) collective-permute-start(bf16[256,512]{1,0:T(8,128)(2,1)S(1)} %get-tuple-element.76), channel_id=1, source_target_pairs={{0,1},{1,2},{2,3},{3,0},{4,5},{5,6},{6,7},{7,4},{8,9},{9,10},{10,1... | collective-permute-start | bytes 786440 | tf_op jit(solution)/shard_map/ppermute | solution.py:227
  67.0 4.8 %collective-permute-done.10.refs_1_ = bf16[256,256]{1,0:T(8,128)(2,1)S(1)} collective-permute-done((bf16[256,256]{1,0:T(8,128)(2,1)S(1)}, bf16[256,256]{1,0:T(8,128)(2,1)S(1)}, u32[]{:S(2)}, u32[]{:S(2)}) %collective-permute-start.10) | collective-permute-done | bytes 131104 | tf_op jit(solution)/shard_map/ppermute | solution.py:227
  72.4 3.2 %collective-permute-start.15 = (bf16[256,512]{1,0:T(8,128)(2,1)S(1)}, bf16[256,512]{1,0:T(8,128)(2,1)S(1)}, u32[]{:S(2)}, u32[]{:S(2)}) collective-permute-start(bf16[256,512]{1,0:T(8,128)(2,1)S(1)} %get-tuple-element.83), channel_id=1, source_target_pairs={{0,1},{1,2},{2,3},{3,0},{4,5},{5,6},{6,7},{7,4},{8,9},{9,10},{10,1... | collective-permute-start | bytes 786440 | tf_op jit(solution)/shard_map/ppermute | solution.py:227
  75.9 2.0 %collective-permute-start.14 = (bf16[256,512]{1,0:T(8,128)(2,1)S(1)}, bf16[256,512]{1,0:T(8,128)(2,1)S(1)}, u32[]{:S(2)}, u32[]{:S(2)}) collective-permute-start(bf16[256,512]{1,0:T(8,128)(2,1)S(1)} %get-tuple-element.81), channel_id=1, source_target_pairs={{0,1},{1,2},{2,3},{3,0},{4,5},{5,6},{6,7},{7,4},{8,9},{9,10},{10,1... | collective-permute-start | bytes 786440 | tf_op jit(solution)/shard_map/ppermute | solution.py:227
  77.9 4.3 %collective-permute-done.12.refs_4_ = bf16[256,512]{1,0:T(8,128)(2,1)S(1)} collective-permute-done((bf16[256,512]{1,0:T(8,128)(2,1)S(1)}, bf16[256,512]{1,0:T(8,128)(2,1)S(1)}, u32[]{:S(2)}, u32[]{:S(2)}) %collective-permute-start.12) | collective-permute-done | bytes 262176 | tf_op jit(solution)/shard_map/ppermute | solution.py:227
  82.6 1.9 %dynamic-slice_bitcast_fusion.4 = bf16[128,2048]{1,0:T(8,128)(2,1)} fusion(bf16[1,2,256,4096]{3,2,1,0:T(8,128)(2,1)} %x_ref.3, s32[]{:T(128)S(6)} %select_n.46), kind=kLoop, calls=%fused_computation.6 | loop fusion | bytes 1048580 | tf_op jit(solution)/shard_map/squeeze | solution.py:265
  85.0 1.9 %dynamic-slice_bitcast_fusion.3 = bf16[128,2048]{1,0:T(8,128)(2,1)} fusion(bf16[1,2,256,4096]{3,2,1,0:T(8,128)(2,1)} %x_ref.3, s32[]{:T(128)S(6)} %select_n.46), kind=kLoop, calls=%fused_computation.5 | loop fusion | bytes 1048580 | tf_op jit(solution)/shard_map/squeeze | solution.py:265
  86.8 1.6 %collective-permute-start.21 = (bf16[128,2048]{1,0:T(8,128)(2,1)}, bf16[128,2048]{1,0:T(8,128)(2,1)S(1)}, u32[]{:S(2)}, u32[]{:S(2)}) collective-permute-start(bf16[128,2048]{1,0:T(8,128)(2,1)} %dynamic-slice_bitcast_fusion.3), channel_id=1, source_target_pairs={{0,4},{1,5},{2,6},{3,7},{4,0},{5,1},{6,2},{7,3},{8,12},{9,13},{10,... | collective-permute-start | bytes 1572872 | tf_op jit(solution)/shard_map/ppermute | solution.py:227
  88.8 3.3 %collective-permute-start.17 = (bf16[256,512]{1,0:T(8,128)(2,1)S(1)}, bf16[256,512]{1,0:T(8,128)(2,1)}, u32[]{:S(2)}, u32[]{:S(2)}) collective-permute-start(bf16[256,512]{1,0:T(8,128)(2,1)S(1)} %get-tuple-element.86.refs_0_.refs_4_), channel_id=1, source_target_pairs={{0,1},{1,2},{2,3},{3,0},{4,5},{5,6},{6,7},{7,4},{8,9},{9,10},{10,1... | collective-permute-start | bytes 786440 | tf_op jit(solution)/shard_map/ppermute | solution.py:227
  92.6 1.0 slice.41
  93.7 1.2 convert_reduce_fusion
  96.5 1.6 %collective-permute-done.17.refs_1_ = bf16[256,512]{1,0:T(8,128)(2,1)} collective-permute-done((bf16[256,512]{1,0:T(8,128)(2,1)S(1)}, bf16[256,512]{1,0:T(8,128)(2,1)}, u32[]{:S(2)}, u32[]{:S(2)}) %collective-permute-start.17) | collective-permute-done | bytes 262176 | tf_op jit(solution)/shard_map/ppermute | solution.py:227
  98.1 3.8 %collective-permute-start.19 = (bf16[256,512]{1,0:T(8,128)(2,1)}, bf16[256,512]{1,0:T(8,128)(2,1)S(1)}, u32[]{:S(2)}, u32[]{:S(2)}) collective-permute-start(bf16[256,512]{1,0:T(8,128)(2,1)} %collective-permute-done.17.refs_1_), channel_id=1, source_target_pairs={{0,1},{1,2},{2,3},{3,0},{4,5},{5,6},{6,7},{7,4},{8,9},{9,10},{10,1... | collective-permute-start | bytes 786440 | tf_op jit(solution)/shard_map/ppermute | solution.py:227
  102.9 1.1 collective-permute-start.24
  103.9 1.9 %collective-permute-done.18.refs_2_ = bf16[256,512]{1,0:T(8,128)(2,1)S(1)} collective-permute-done((bf16[256,512]{1,0:T(8,128)(2,1)S(1)}, bf16[256,512]{1,0:T(8,128)(2,1)S(1)}, u32[]{:S(2)}, u32[]{:S(2)}) %collective-permute-start.18) | collective-permute-done | bytes 262176 | tf_op jit(solution)/shard_map/ppermute | solution.py:227
  105.8 1.6 %collective-permute-done.21.refs_5_.refs_4_.refs_12_ = bf16[128,2048]{1,0:T(8,128)(2,1)S(1)} collective-permute-done((bf16[128,2048]{1,0:T(8,128)(2,1)}, bf16[128,2048]{1,0:T(8,128)(2,1)S(1)}, u32[]{:S(2)}, u32[]{:S(2)}) %collective-permute-start.21) | collective-permute-done | bytes 524320 | tf_op jit(solution)/shard_map/ppermute | solution.py:227
  107.4 1.7 %value_partial.6 = (bf16[256,256]{1,0:T(8,128)(2,1)S(1)}, f32[8,128]{1,0:T(8,128)S(1)}) custom-call(s32[1]{0:T(128)} %bitcast.x_at, f32[8,128]{1,0:T(8,128)S(1)} %get-tuple-element.85.token_in, bf16[256,512]{1,0:T(8,128)(2,1)S(1)} %get-tuple-element.86.refs_0_.refs_4_, bf16[256,512]{1,0:T(8,128)(2,1)} %collective-permute-done.17.refs_1_, ...), custom_call_target="tpu_custom_call" | custom-call | flops 1000 | bytes 1000 | tf_op jit(solution)/shard_map/value_partial/pallas_call | solution.py:131
  109.2 1.2 collective-permute-done.24.refs_3_
  111.2 0.8 collective-permute-start.26
  112.0 1.3 dynamic-slice_bitcast_fusion.refs_4_.refs_2_.refs_10_
  113.4 0.8 collective-permute-done.25.refs_5_
  114.2 1.0 copy-done.1
  115.2 1.6 %grad_value.6 = (bf16[256,256]{1,0:T(8,128)(2,1)S(1)}, f32[8,128]{1,0:T(8,128)S(1)}) custom-call(s32[1]{0:T(128)} %bitcast.x_at, f32[8,128]{1,0:T(8,128)S(1)} %get-tuple-element.91.token_in, bf16[256,512]{1,0:T(8,128)(2,1)S(1)} %get-tuple-element.86.refs_0_.refs_4_, bf16[256,512]{1,0:T(8,128)(2,1)} %collective-permute-done.17.refs_1_, ...), custom_call_target="tpu_custom_call" | custom-call | flops 1000 | bytes 1000 | tf_op jit(solution)/shard_map/grad_value/pallas_call | solution.py:131
  117.4 0.9 copy-done.6
  119.0 1.6 %collective-permute-start.28 = (bf16[256,256]{1,0:T(8,128)(2,1)S(1)}, bf16[256,256]{1,0:T(8,128)(2,1)S(1)}, u32[]{:S(2)}, u32[]{:S(2)}) collective-permute-start(bf16[256,256]{1,0:T(8,128)(2,1)S(1)} %get-tuple-element.100.refs_0_.refs_5_), channel_id=1, source_target_pairs={{0,4},{1,5},{2,6},{3,7},{4,0},{5,1},{6,2},{7,3},{8,12},{9,13},{10,... | collective-permute-start | bytes 393224 | tf_op jit(solution)/shard_map/ppermute | solution.py:227
  120.7 1.2 collective-permute-done.27.refs_1_
  121.9 1.1 sum_partial.6
  123.0 3.7 %collective-permute-start.29 = (bf16[256,512]{1,0:T(8,128)(2,1)}, bf16[256,512]{1,0:T(8,128)(2,1)}, u32[]{:S(2)}, u32[]{:S(2)}) collective-permute-start(bf16[256,512]{1,0:T(8,128)(2,1)} %get-tuple-element.102), channel_id=1, source_target_pairs={{0,1},{1,2},{2,3},{3,0},{4,5},{5,6},{6,7},{7,4},{8,9},{9,10},{10,1... | collective-permute-start | bytes 786440 | tf_op jit(solution)/shard_map/ppermute | solution.py:227
  126.6 1.1 sum_partial.7
  128.4 3.3 %collective-permute-start.33 = (bf16[256,512]{1,0:T(8,128)(2,1)}, bf16[256,512]{1,0:T(8,128)(2,1)S(1)}, u32[]{:S(2)}, u32[]{:S(2)}) collective-permute-start(bf16[256,512]{1,0:T(8,128)(2,1)} %copy-done.15), channel_id=1, source_target_pairs={{0,1},{1,2},{2,3},{3,0},{4,5},{5,6},{6,7},{7,4},{8,9},{9,10},{10,1... | collective-permute-start | bytes 786440 | tf_op jit(solution)/shard_map/ppermute | solution.py:227
  131.7 2.0 %collective-permute-done.29.refs_5_ = bf16[256,512]{1,0:T(8,128)(2,1)} collective-permute-done((bf16[256,512]{1,0:T(8,128)(2,1)}, bf16[256,512]{1,0:T(8,128)(2,1)}, u32[]{:S(2)}, u32[]{:S(2)}) %collective-permute-start.29) | collective-permute-done | bytes 262176 | tf_op jit(solution)/shard_map/ppermute | solution.py:227
  133.7 1.3 sum_added.6
  135.0 3.8 %collective-permute-start.32 = (bf16[256,512]{1,0:T(8,128)(2,1)S(1)}, bf16[256,512]{1,0:T(8,128)(2,1)S(1)}, u32[]{:S(2)}, u32[]{:S(2)}) collective-permute-start(bf16[256,512]{1,0:T(8,128)(2,1)S(1)} %get-tuple-element.107), channel_id=1, source_target_pairs={{0,1},{1,2},{2,3},{3,0},{4,5},{5,6},{6,7},{7,4},{8,9},{9,10},{10,1... | collective-permute-start | bytes 786440 | tf_op jit(solution)/shard_map/ppermute | solution.py:227
  141.8 0.9 collective-permute-done.32.refs_3_
  143.4 3.4 %collective-permute-done.34.refs_8_ = bf16[256,512]{1,0:T(8,128)(2,1)S(1)} collective-permute-done((bf16[256,512]{1,0:T(8,128)(2,1)S(1)}, bf16[256,512]{1,0:T(8,128)(2,1)S(1)}, u32[]{:S(2)}, u32[]{:S(2)}) %collective-permute-start.34) | collective-permute-done | bytes 262176 | tf_op jit(solution)/shard_map/ppermute | solution.py:227
  146.8 1.2 copy-done.4
  148.0 0.9 copy-done.8
  149.0 0.9 copy-done.10
  149.9 0.9 copy-done.12
  150.9 1.9 %last_step.1 = (bf16[1,512,512]{2,1,0:T(8,128)(2,1)}, bf16[1,512,512]{2,1,0:T(8,128)(2,1)}, f32[8,128]{1,0:T(8,128)}) custom-call(s32[1]{0:T(128)} %bitcast.x_at, f32[8,128]{1,0:T(8,128)S(1)} %get-tuple-element.105.token_in, bf16[256,256]{1,0:T(8,128)(2,1)S(1)} %get-tuple-element.98.refs_0_, bf16[256,256]{1,0:T(8,128)(2,1)S(1)} %collective-permute-done.27.refs_1_, ...), custom_call_target="tpu_custom_call" | custom-call | flops 1000 | bytes 1000 | tf_op jit(solution)/shard_map/last_step/pallas_call | solution.py:131
  (109 shorter events, 17.1 us)
Async XLA Ops:
  7.2 36.6 %reduce-scatter.2.cloned.1.call-start = ((), (), s32[]{:S(2)}) async-start(), calls=%async_computation.1 | async-start | bytes 655360 | tf_op jit(solution)/shard_map/reduce_scatter | solution.py:346
  9.5 29.9 %collective-permute-start.3 = (bf16[256,2048]{1,0:T(8,128)(2,1)}, bf16[256,2048]{1,0:T(8,128)(2,1)S(1)}, u32[]{:S(2)}, u32[]{:S(2)}) collective-permute-start(bf16[256,2048]{1,0:T(8,128)(2,1)} %dynamic-slice_bitcast_fusion.2._), channel_id=1, source_target_pairs={{0,4},{1,5},{2,6},{3,7},{4,0},{5,1},{6,2},{7,3},{8,12},{9,13},{10,... | collective-permute-start | bytes 3145736 | tf_op jit(solution)/shard_map/ppermute | solution.py:227
  13.3 79.3 %all-gather.6.cloned.1.call-start = ((), (), s32[]{:S(2)}) async-start(), calls=%async_computation.3 | async-start | bytes 1310720 | tf_op jit(solution)/shard_map/all_gather | solution.py:343
  14.5 11.4 %collective-permute-start = (bf16[256,512]{1,0:T(8,128)(2,1)S(1)}, bf16[256,512]{1,0:T(8,128)(2,1)S(1)}, u32[]{:S(2)}, u32[]{:S(2)}) collective-permute-start(bf16[256,512]{1,0:T(8,128)(2,1)S(1)} %get-tuple-element.119.refs_0_.refs_6_), channel_id=1, source_target_pairs={{0,1},{1,2},{2,3},{3,0},{4,5},{5,6},{6,7},{7,4},{8,9},{9,10},{10,1... | collective-permute-start | bytes 786440 | tf_op jit(solution)/shard_map/ppermute | solution.py:227
  15.0 13.8 %collective-permute-start.5 = (bf16[256,512]{1,0:T(8,128)(2,1)S(1)}, bf16[256,512]{1,0:T(8,128)(2,1)S(1)}, u32[]{:S(2)}, u32[]{:S(2)}) collective-permute-start(bf16[256,512]{1,0:T(8,128)(2,1)S(1)} %get-tuple-element.118.refs_0_.refs_6_), channel_id=1, source_target_pairs={{0,3},{1,0},{2,1},{3,2},{4,7},{5,4},{6,5},{7,6},{8,11},{9,8},{10,9... | collective-permute-start | bytes 786440 | tf_op jit(solution)/shard_map/ppermute | solution.py:227
  16.6 22.9 %collective-permute-start.1 = (bf16[256,512]{1,0:T(8,128)(2,1)S(1)}, bf16[256,512]{1,0:T(8,128)(2,1)}, u32[]{:S(2)}, u32[]{:S(2)}) collective-permute-start(bf16[256,512]{1,0:T(8,128)(2,1)S(1)} %get-tuple-element.119.refs_0_.refs_6_), channel_id=1, source_target_pairs={{0,3},{1,0},{2,1},{3,2},{4,7},{5,4},{6,5},{7,6},{8,11},{9,8},{10,9... | collective-permute-start | bytes 786440 | tf_op jit(solution)/shard_map/ppermute | solution.py:227
  25.8 12.4 %copy-start.19 = (f32[16,512]{1,0:T(8,128)S(1)}, f32[16,512]{1,0:T(8,128)}, u32[]{:S(2)}) copy-start(f32[16,512]{1,0:T(8,128)} %param.12) | copy-start | bytes 98308
  25.8 13.0 %copy-start.21 = (f32[16,512]{1,0:T(8,128)S(1)}, f32[16,512]{1,0:T(8,128)}, u32[]{:S(2)}) copy-start(f32[16,512]{1,0:T(8,128)} %param.11) | copy-start | bytes 98308
  25.8 13.6 %collective-permute-start.2 = (bf16[256,512]{1,0:T(8,128)(2,1)S(1)}, bf16[256,512]{1,0:T(8,128)(2,1)}, u32[]{:S(2)}, u32[]{:S(2)}) collective-permute-start(bf16[256,512]{1,0:T(8,128)(2,1)S(1)} %collective-permute-done.refs_1_), channel_id=1, source_target_pairs={{0,1},{1,2},{2,3},{3,0},{4,5},{5,6},{6,7},{7,4},{8,9},{9,10},{10,1... | collective-permute-start | bytes 786440 | tf_op jit(solution)/shard_map/ppermute | solution.py:227
  28.3 13.3 %collective-permute-start.4 = (bf16[256,512]{1,0:T(8,128)(2,1)S(1)}, bf16[256,512]{1,0:T(8,128)(2,1)S(1)}, u32[]{:S(2)}, u32[]{:S(2)}) collective-permute-start(bf16[256,512]{1,0:T(8,128)(2,1)S(1)} %get-tuple-element.118.refs_0_.refs_6_), channel_id=1, source_target_pairs={{0,1},{1,2},{2,3},{3,0},{4,5},{5,6},{6,7},{7,4},{8,9},{9,10},{10,1... | collective-permute-start | bytes 786440 | tf_op jit(solution)/shard_map/ppermute | solution.py:227
  28.8 12.8 %collective-permute-start.6 = (bf16[256,512]{1,0:T(8,128)(2,1)S(1)}, bf16[256,512]{1,0:T(8,128)(2,1)}, u32[]{:S(2)}, u32[]{:S(2)}) collective-permute-start(bf16[256,512]{1,0:T(8,128)(2,1)S(1)} %collective-permute-done.5.refs_2_), channel_id=1, source_target_pairs={{0,3},{1,0},{2,1},{3,2},{4,7},{5,4},{6,5},{7,6},{8,11},{9,8},{10,9... | collective-permute-start | bytes 786440 | tf_op jit(solution)/shard_map/ppermute | solution.py:227
  38.2 18.2 %copy-start.2 = (bf16[4,256,256]{2,1,0:T(8,128)(2,1)S(1)}, bf16[4,256,256]{2,1,0:T(8,128)(2,1)}, u32[]{:S(2)}) copy-start(bf16[4,256,256]{2,1,0:T(8,128)(2,1)} %get-tuple-element.67.refs_6_) | copy-start | bytes 1572868
  38.2 18.2 %copy-start.3 = (f32[512,256]{1,0:T(8,128)S(1)}, f32[512,256]{1,0:T(8,128)}, u32[]{:S(2)}) copy-start(f32[512,256]{1,0:T(8,128)} %get-tuple-element.68.refs_7_) | copy-start | bytes 1572868
  39.5 0.7 copy-start.13
  41.6 0.7 copy-start.16
  45.3 1.7 %collective-permute-start.35 = (bf16[160,512]{1,0:T(8,128)(2,1)}, bf16[160,512]{1,0:T(8,128)(2,1)}, u32[]{:S(2)}, u32[]{:S(2)}) collective-permute-start(bf16[160,512]{1,0:T(8,128)(2,1)} %pad_maximum_fusion.1), channel_id=1, source_target_pairs={{0,8},{8,0},{16,24},{24,16},{32,40},{40,32},{48,56},{56,48},{64,72... | collective-permute-start | bytes 491528 | tf_op jit(solution)/shard_map/ppermute | solution.py:357
  49.7 97.1 %all-gather.4.cloned.1.call-start = ((), (), s32[]{:S(2)}) async-start(), calls=%async_computation.2 | async-start | bytes 1310720 | tf_op jit(solution)/shard_map/all_gather | solution.py:343
  49.7 6.6 %collective-permute-start.7 = (bf16[256,256]{1,0:T(8,128)(2,1)}, bf16[256,256]{1,0:T(8,128)(2,1)S(1)}, u32[]{:S(2)}, u32[]{:S(2)}) collective-permute-start(bf16[256,256]{1,0:T(8,128)(2,1)} %copy-done.16), channel_id=1, source_target_pairs={{0,4},{1,5},{2,6},{3,7},{4,0},{5,1},{6,2},{7,3},{8,12},{9,13},{10,... | collective-permute-start | bytes 393224 | tf_op jit(solution)/shard_map/ppermute | solution.py:227
  49.9 8.5 %collective-permute-start.8 = (bf16[256,256]{1,0:T(8,128)(2,1)S(1)}, bf16[256,256]{1,0:T(8,128)(2,1)S(1)}, u32[]{:S(2)}, u32[]{:S(2)}) collective-permute-start(bf16[256,256]{1,0:T(8,128)(2,1)S(1)} %get-tuple-element.70), channel_id=1, source_target_pairs={{0,4},{1,5},{2,6},{3,7},{4,0},{5,1},{6,2},{7,3},{8,12},{9,13},{10,... | collective-permute-start | bytes 393224 | tf_op jit(solution)/shard_map/ppermute | solution.py:227
  58.1 6.5 %collective-permute-start.9 = (bf16[256,256]{1,0:T(8,128)(2,1)S(1)}, bf16[256,256]{1,0:T(8,128)(2,1)S(1)}, u32[]{:S(2)}, u32[]{:S(2)}) collective-permute-start(bf16[256,256]{1,0:T(8,128)(2,1)S(1)} %get-tuple-element.72.refs_0_), channel_id=1, source_target_pairs={{0,4},{1,5},{2,6},{3,7},{4,0},{5,1},{6,2},{7,3},{8,12},{9,13},{10,... | collective-permute-start | bytes 393224 | tf_op jit(solution)/shard_map/ppermute | solution.py:227
  60.1 11.7 %collective-permute-start.10 = (bf16[256,256]{1,0:T(8,128)(2,1)S(1)}, bf16[256,256]{1,0:T(8,128)(2,1)S(1)}, u32[]{:S(2)}, u32[]{:S(2)}) collective-permute-start(bf16[256,256]{1,0:T(8,128)(2,1)S(1)} %get-tuple-element.74.refs_0_), channel_id=1, source_target_pairs={{0,4},{1,5},{2,6},{3,7},{4,0},{5,1},{6,2},{7,3},{8,12},{9,13},{10,... | collective-permute-start | bytes 393224 | tf_op jit(solution)/shard_map/ppermute | solution.py:227
  65.1 10.5 %collective-permute-start.11 = (bf16[256,512]{1,0:T(8,128)(2,1)S(1)}, bf16[256,512]{1,0:T(8,128)(2,1)S(1)}, u32[]{:S(2)}, u32[]{:S(2)}) collective-permute-start(bf16[256,512]{1,0:T(8,128)(2,1)S(1)} %get-tuple-element.76), channel_id=1, source_target_pairs={{0,1},{1,2},{2,3},{3,0},{4,5},{5,6},{6,7},{7,4},{8,9},{9,10},{10,1... | collective-permute-start | bytes 786440 | tf_op jit(solution)/shard_map/ppermute | solution.py:227
  72.2 10.0 %collective-permute-start.12 = (bf16[256,512]{1,0:T(8,128)(2,1)S(1)}, bf16[256,512]{1,0:T(8,128)(2,1)S(1)}, u32[]{:S(2)}, u32[]{:S(2)}) collective-permute-start(bf16[256,512]{1,0:T(8,128)(2,1)S(1)} %get-tuple-element.78), channel_id=1, source_target_pairs={{0,3},{1,0},{2,1},{3,2},{4,7},{5,4},{6,5},{7,6},{8,11},{9,8},{10,9... | collective-permute-start | bytes 786440 | tf_op jit(solution)/shard_map/ppermute | solution.py:227
  72.3 14.5 %collective-permute-start.13 = (bf16[256,512]{1,0:T(8,128)(2,1)S(1)}, bf16[256,512]{1,0:T(8,128)(2,1)S(1)}, u32[]{:S(2)}, u32[]{:S(2)}) collective-permute-start(bf16[256,512]{1,0:T(8,128)(2,1)S(1)} %get-tuple-element.80), channel_id=1, source_target_pairs={{0,3},{1,0},{2,1},{3,2},{4,7},{5,4},{6,5},{7,6},{8,11},{9,8},{10,9... | collective-permute-start | bytes 786440 | tf_op jit(solution)/shard_map/ppermute | solution.py:227
  72.4 19.7 %collective-permute-start.15 = (bf16[256,512]{1,0:T(8,128)(2,1)S(1)}, bf16[256,512]{1,0:T(8,128)(2,1)S(1)}, u32[]{:S(2)}, u32[]{:S(2)}) collective-permute-start(bf16[256,512]{1,0:T(8,128)(2,1)S(1)} %get-tuple-element.83), channel_id=1, source_target_pairs={{0,1},{1,2},{2,3},{3,0},{4,5},{5,6},{6,7},{7,4},{8,9},{9,10},{10,1... | collective-permute-start | bytes 786440 | tf_op jit(solution)/shard_map/ppermute | solution.py:227
  75.9 12.5 %collective-permute-start.14 = (bf16[256,512]{1,0:T(8,128)(2,1)S(1)}, bf16[256,512]{1,0:T(8,128)(2,1)S(1)}, u32[]{:S(2)}, u32[]{:S(2)}) collective-permute-start(bf16[256,512]{1,0:T(8,128)(2,1)S(1)} %get-tuple-element.81), channel_id=1, source_target_pairs={{0,1},{1,2},{2,3},{3,0},{4,5},{5,6},{6,7},{7,4},{8,9},{9,10},{10,1... | collective-permute-start | bytes 786440 | tf_op jit(solution)/shard_map/ppermute | solution.py:227
  82.6 9.6 %collective-permute-start.16 = (bf16[256,512]{1,0:T(8,128)(2,1)S(1)}, bf16[256,512]{1,0:T(8,128)(2,1)S(1)}, u32[]{:S(2)}, u32[]{:S(2)}) collective-permute-start(bf16[256,512]{1,0:T(8,128)(2,1)S(1)} %get-tuple-element.84), channel_id=1, source_target_pairs={{0,3},{1,0},{2,1},{3,2},{4,7},{5,4},{6,5},{7,6},{8,11},{9,8},{10,9... | collective-permute-start | bytes 786440 | tf_op jit(solution)/shard_map/ppermute | solution.py:227
  84.5 17.4 %collective-permute-start.20 = (bf16[128,2048]{1,0:T(8,128)(2,1)}, bf16[128,2048]{1,0:T(8,128)(2,1)S(1)}, u32[]{:S(2)}, u32[]{:S(2)}) collective-permute-start(bf16[128,2048]{1,0:T(8,128)(2,1)} %dynamic-slice_bitcast_fusion.4), channel_id=1, source_target_pairs={{0,4},{1,5},{2,6},{3,7},{4,0},{5,1},{6,2},{7,3},{8,12},{9,13},{10,... | collective-permute-start | bytes 1572872 | tf_op jit(solution)/shard_map/ppermute | solution.py:227
  86.8 20.6 %collective-permute-start.21 = (bf16[128,2048]{1,0:T(8,128)(2,1)}, bf16[128,2048]{1,0:T(8,128)(2,1)S(1)}, u32[]{:S(2)}, u32[]{:S(2)}) collective-permute-start(bf16[128,2048]{1,0:T(8,128)(2,1)} %dynamic-slice_bitcast_fusion.3), channel_id=1, source_target_pairs={{0,4},{1,5},{2,6},{3,7},{4,0},{5,1},{6,2},{7,3},{8,12},{9,13},{10,... | collective-permute-start | bytes 1572872 | tf_op jit(solution)/shard_map/ppermute | solution.py:227
  88.8 9.3 %collective-permute-start.17 = (bf16[256,512]{1,0:T(8,128)(2,1)S(1)}, bf16[256,512]{1,0:T(8,128)(2,1)}, u32[]{:S(2)}, u32[]{:S(2)}) collective-permute-start(bf16[256,512]{1,0:T(8,128)(2,1)S(1)} %get-tuple-element.86.refs_0_.refs_4_), channel_id=1, source_target_pairs={{0,1},{1,2},{2,3},{3,0},{4,5},{5,6},{6,7},{7,4},{8,9},{9,10},{10,1... | collective-permute-start | bytes 786440 | tf_op jit(solution)/shard_map/ppermute | solution.py:227
  92.5 10.4 %collective-permute-start.23 = (bf16[256,512]{1,0:T(8,128)(2,1)S(1)}, bf16[256,512]{1,0:T(8,128)(2,1)S(1)}, u32[]{:S(2)}, u32[]{:S(2)}) collective-permute-start(bf16[256,512]{1,0:T(8,128)(2,1)S(1)} %get-tuple-element.90.refs_0_.refs_9_), channel_id=1, source_target_pairs={{0,3},{1,0},{2,1},{3,2},{4,7},{5,4},{6,5},{7,6},{8,11},{9,8},{10,9... | collective-permute-start | bytes 786440 | tf_op jit(solution)/shard_map/ppermute | solution.py:227
  94.9 0.7 copy-start.17
  94.9 19.2 %copy-start = (bf16[4,256,256]{2,1,0:T(8,128)(2,1)S(1)}, bf16[4,256,256]{2,1,0:T(8,128)(2,1)}, u32[]{:S(2)}) copy-start(bf16[4,256,256]{2,1,0:T(8,128)(2,1)} %get-tuple-element.93.refs_6_) | copy-start | bytes 1572868
  96.4 9.4 %collective-permute-start.18 = (bf16[256,512]{1,0:T(8,128)(2,1)S(1)}, bf16[256,512]{1,0:T(8,128)(2,1)S(1)}, u32[]{:S(2)}, u32[]{:S(2)}) collective-permute-start(bf16[256,512]{1,0:T(8,128)(2,1)S(1)} %get-tuple-element.86.refs_0_.refs_4_), channel_id=1, source_target_pairs={{0,3},{1,0},{2,1},{3,2},{4,7},{5,4},{6,5},{7,6},{8,11},{9,8},{10,9... | collective-permute-start | bytes 786440 | tf_op jit(solution)/shard_map/ppermute | solution.py:227
  98.1 9.3 %collective-permute-start.19 = (bf16[256,512]{1,0:T(8,128)(2,1)}, bf16[256,512]{1,0:T(8,128)(2,1)S(1)}, u32[]{:S(2)}, u32[]{:S(2)}) collective-permute-start(bf16[256,512]{1,0:T(8,128)(2,1)} %collective-permute-done.17.refs_1_), channel_id=1, source_target_pairs={{0,1},{1,2},{2,3},{3,0},{4,5},{5,6},{6,7},{7,4},{8,9},{9,10},{10,1... | collective-permute-start | bytes 786440 | tf_op jit(solution)/shard_map/ppermute | solution.py:227
  101.9 7.3 %collective-permute-start.22 = (bf16[256,512]{1,0:T(8,128)(2,1)S(1)}, bf16[256,512]{1,0:T(8,128)(2,1)S(1)}, u32[]{:S(2)}, u32[]{:S(2)}) collective-permute-start(bf16[256,512]{1,0:T(8,128)(2,1)S(1)} %get-tuple-element.90.refs_0_.refs_9_), channel_id=1, source_target_pairs={{0,1},{1,2},{2,3},{3,0},{4,5},{5,6},{6,7},{7,4},{8,9},{9,10},{10,1... | collective-permute-start | bytes 786440 | tf_op jit(solution)/shard_map/ppermute | solution.py:227
  102.9 11.3 %copy-start.5 = (bf16[256,512]{1,0:T(8,128)(2,1)}, bf16[256,512]{1,0:T(8,128)(2,1)S(1)}, u32[]{:S(2)}) copy-start(bf16[256,512]{1,0:T(8,128)(2,1)S(1)} %collective-permute-done.23.refs_2_) | copy-start | bytes 786436
  102.9 7.6 %collective-permute-start.24 = (bf16[256,512]{1,0:T(8,128)(2,1)S(1)}, bf16[256,512]{1,0:T(8,128)(2,1)S(1)}, u32[]{:S(2)}, u32[]{:S(2)}) collective-permute-start(bf16[256,512]{1,0:T(8,128)(2,1)S(1)} %collective-permute-done.23.refs_2_), channel_id=1, source_target_pairs={{0,3},{1,0},{2,1},{3,2},{4,7},{5,4},{6,5},{7,6},{8,11},{9,8},{10,9... | collective-permute-start | bytes 786440 | tf_op jit(solution)/shard_map/ppermute | solution.py:227
  109.1 5.1 %collective-permute-start.25 = (bf16[256,256]{1,0:T(8,128)(2,1)S(1)}, bf16[256,256]{1,0:T(8,128)(2,1)S(1)}, u32[]{:S(2)}, u32[]{:S(2)}) collective-permute-start(bf16[256,256]{1,0:T(8,128)(2,1)S(1)} %get-tuple-element.92), channel_id=1, source_target_pairs={{0,4},{1,5},{2,6},{3,7},{4,0},{5,1},{6,2},{7,3},{8,12},{9,13},{10,... | collective-permute-start | bytes 393224 | tf_op jit(solution)/shard_map/ppermute | solution.py:227
  111.2 6.2 %collective-permute-start.26 = (bf16[256,256]{1,0:T(8,128)(2,1)S(1)}, bf16[256,256]{1,0:T(8,128)(2,1)S(1)}, u32[]{:S(2)}, u32[]{:S(2)}) collective-permute-start(bf16[256,256]{1,0:T(8,128)(2,1)S(1)} %get-tuple-element.96), channel_id=1, source_target_pairs={{0,4},{1,5},{2,6},{3,7},{4,0},{5,1},{6,2},{7,3},{8,12},{9,13},{10,... | collective-permute-start | bytes 393224 | tf_op jit(solution)/shard_map/ppermute | solution.py:227
  114.2 1.0 copy-start.1
  116.8 5.1 %collective-permute-start.27 = (bf16[256,256]{1,0:T(8,128)(2,1)S(1)}, bf16[256,256]{1,0:T(8,128)(2,1)S(1)}, u32[]{:S(2)}, u32[]{:S(2)}) collective-permute-start(bf16[256,256]{1,0:T(8,128)(2,1)S(1)} %get-tuple-element.98.refs_0_), channel_id=1, source_target_pairs={{0,4},{1,5},{2,6},{3,7},{4,0},{5,1},{6,2},{7,3},{8,12},{9,13},{10,... | collective-permute-start | bytes 393224 | tf_op jit(solution)/shard_map/ppermute | solution.py:227
  117.4 1.0 copy-start.6
  119.0 7.6 %collective-permute-start.28 = (bf16[256,256]{1,0:T(8,128)(2,1)S(1)}, bf16[256,256]{1,0:T(8,128)(2,1)S(1)}, u32[]{:S(2)}, u32[]{:S(2)}) collective-permute-start(bf16[256,256]{1,0:T(8,128)(2,1)S(1)} %get-tuple-element.100.refs_0_.refs_5_), channel_id=1, source_target_pairs={{0,4},{1,5},{2,6},{3,7},{4,0},{5,1},{6,2},{7,3},{8,12},{9,13},{10,... | collective-permute-start | bytes 393224 | tf_op jit(solution)/shard_map/ppermute | solution.py:227
  122.9 4.7 %copy-start.14 = (bf16[256,512]{1,0:T(8,128)(2,1)}, bf16[256,512]{1,0:T(8,128)(2,1)S(1)}, u32[]{:S(2)}) copy-start(bf16[256,512]{1,0:T(8,128)(2,1)S(1)} %get-tuple-element.106) | copy-start | bytes 786436
  123.0 16.3 %copy-start.20 = (f32[16,512]{1,0:T(8,128)S(1)}, f32[16,512]{1,0:T(8,128)}, u32[]{:S(2)}) copy-start(f32[16,512]{1,0:T(8,128)} %param.12) | copy-start | bytes 98308
  123.0 16.3 %copy-start.22 = (f32[16,512]{1,0:T(8,128)S(1)}, f32[16,512]{1,0:T(8,128)}, u32[]{:S(2)}) copy-start(f32[16,512]{1,0:T(8,128)} %param.11) | copy-start | bytes 98308
  123.0 10.7 %collective-permute-start.29 = (bf16[256,512]{1,0:T(8,128)(2,1)}, bf16[256,512]{1,0:T(8,128)(2,1)}, u32[]{:S(2)}, u32[]{:S(2)}) collective-permute-start(bf16[256,512]{1,0:T(8,128)(2,1)} %get-tuple-element.102), channel_id=1, source_target_pairs={{0,1},{1,2},{2,3},{3,0},{4,5},{5,6},{6,7},{7,4},{8,9},{9,10},{10,1... | collective-permute-start | bytes 786440 | tf_op jit(solution)/shard_map/ppermute | solution.py:227
  127.7 0.7 copy-start.15
  128.4 10.4 %collective-permute-start.30 = (bf16[256,512]{1,0:T(8,128)(2,1)}, bf16[256,512]{1,0:T(8,128)(2,1)S(1)}, u32[]{:S(2)}, u32[]{:S(2)}) collective-permute-start(bf16[256,512]{1,0:T(8,128)(2,1)} %get-tuple-element.104), channel_id=1, source_target_pairs={{0,3},{1,0},{2,1},{3,2},{4,7},{5,4},{6,5},{7,6},{8,11},{9,8},{10,9... | collective-permute-start | bytes 786440 | tf_op jit(solution)/shard_map/ppermute | solution.py:227
  128.4 10.8 %copy-start.18 = (f32[128,512]{1,0:T(8,128)S(1)}, f32[128,512]{1,0:T(8,128)}, u32[]{:S(2)}) copy-start(f32[128,512]{1,0:T(8,128)} %copy-done.17) | copy-start | bytes 786436
  128.4 11.9 %collective-permute-start.31 = (bf16[256,512]{1,0:T(8,128)(2,1)}, bf16[256,512]{1,0:T(8,128)(2,1)S(1)}, u32[]{:S(2)}, u32[]{:S(2)}) collective-permute-start(bf16[256,512]{1,0:T(8,128)(2,1)} %copy-done.14), channel_id=1, source_target_pairs={{0,3},{1,0},{2,1},{3,2},{4,7},{5,4},{6,5},{7,6},{8,11},{9,8},{10,9... | collective-permute-start | bytes 786440 | tf_op jit(solution)/shard_map/ppermute | solution.py:227
  128.4 12.6 %collective-permute-start.33 = (bf16[256,512]{1,0:T(8,128)(2,1)}, bf16[256,512]{1,0:T(8,128)(2,1)S(1)}, u32[]{:S(2)}, u32[]{:S(2)}) collective-permute-start(bf16[256,512]{1,0:T(8,128)(2,1)} %copy-done.15), channel_id=1, source_target_pairs={{0,1},{1,2},{2,3},{3,0},{4,5},{5,6},{6,7},{7,4},{8,9},{9,10},{10,1... | collective-permute-start | bytes 786440 | tf_op jit(solution)/shard_map/ppermute | solution.py:227
  135.0 7.7 %collective-permute-start.32 = (bf16[256,512]{1,0:T(8,128)(2,1)S(1)}, bf16[256,512]{1,0:T(8,128)(2,1)S(1)}, u32[]{:S(2)}, u32[]{:S(2)}) collective-permute-start(bf16[256,512]{1,0:T(8,128)(2,1)S(1)} %get-tuple-element.107), channel_id=1, source_target_pairs={{0,1},{1,2},{2,3},{3,0},{4,5},{5,6},{6,7},{7,4},{8,9},{9,10},{10,1... | collective-permute-start | bytes 786440 | tf_op jit(solution)/shard_map/ppermute | solution.py:227
  139.1 7.7 %collective-permute-start.34 = (bf16[256,512]{1,0:T(8,128)(2,1)S(1)}, bf16[256,512]{1,0:T(8,128)(2,1)S(1)}, u32[]{:S(2)}, u32[]{:S(2)}) collective-permute-start(bf16[256,512]{1,0:T(8,128)(2,1)S(1)} %get-tuple-element.109), channel_id=1, source_target_pairs={{0,3},{1,0},{2,1},{3,2},{4,7},{5,4},{6,5},{7,6},{8,11},{9,8},{10,9... | collective-permute-start | bytes 786440 | tf_op jit(solution)/shard_map/ppermute | solution.py:227
  140.3 0.7 copy-start.7
  141.0 0.7 copy-start.9
  142.7 0.7 copy-start.11
  146.8 1.2 copy-start.4
  148.0 0.9 copy-start.8
  149.0 0.9 copy-start.10
  149.9 0.9 copy-start.12
Sparse Core Ops, SparseCore 0:
  13.5 22.8 reduce-scatter.1
  49.8 36.9 all-gather.5
  96.5 29.8 all-gather.3
